TPU v7x, 128 devices: a whole 4x4x4 slice. The times are simulated.
128 devices in a mesh: wide: 16 (over z, x), narrow: 8 (over y, core).
Axes of the slice: x: 4, y: 4, z: 4, core: 2. Of those that a mesh axis runs over, the one named last changes fastest.
Arguments:
- points: bfloat16 [131072, 1024], P(('wide', 'narrow')), may hold values from -8 to 8
- block_bucket: int32 [65536], P(('wide', 'narrow')), may hold values from 0 to 511, as said below
- fine: bfloat16 [262144, 1024], P(('wide', 'narrow')), may hold values from -8 to 8
- sharp: float32 [512], P(('wide', 'narrow')), may hold values from 0.5 to 4
- parents: int32 [262144], P(('wide', 'narrow')), may hold values from 0 to 4095, as said below
- coarse_old: bfloat16 [4096, 1024], P(('wide', 'narrow')), may hold values from -6 to 6
Outputs:
- fine_new: bfloat16 [262144, 1024], P(('wide', 'narrow'))
- coarse_new: bfloat16 [4096, 1024], P(('wide', 'narrow'))
- point_entropy: float32 [131072], P(('wide', 'narrow'))
Inputs may be any that keep to these rules, and one draw needn't show every extreme that they name: `block_bucket`: among the 512 blocks of one device no bucket is named more than 2 times, and one bucket is named exactly 2 times by the blocks of every device. `parents`: the parent of fine centroid j is one of the 256 coarse centroids from (j // 16384) * 256 on.
All inputs are finite; a program needn't handle non-finite values.
Results may differ from a plain program's by a relative error of at most 0.0085.
Values may be sent and summed in bfloat16 or wider, within the bound.
A program may use at most 128 MiB of HBM per device.

v0:
```python
import jax
import jax.numpy as jnp
from jax import lax
from jax.sharding import PartitionSpec as P

CAP = 2


PRIOR_MASS = 1.0


def soft_assign(row_data, row_live, centroids, sharpness):
    scale_factor = centroids.shape[1] ** (-0.5)
    products = jnp.einsum("rd,kd->rk", row_data, centroids, preferred_element_type=jnp.float32)
    cent_float = centroids.astype(jnp.float32)
    sq_norms = jnp.sum(cent_float * cent_float, axis=1)
    logits = sharpness * (products - 0.5 * sq_norms[None, :]) * scale_factor
    highest = jnp.max(logits, axis=1, keepdims=True)
    shifted = logits - highest
    exponent = jnp.exp(shifted)
    totals = jnp.sum(exponent, axis=1, keepdims=True)
    probability = exponent / totals
    entropy = jnp.log(totals[:, 0]) - jnp.sum(probability * shifted, axis=1)
    weights = (probability * row_live[:, None]).astype(jnp.bfloat16)
    masses = jnp.sum(weights.astype(jnp.float32), axis=0)
    weighted = jnp.einsum("rk,rd->kd", weights, row_data, preferred_element_type=jnp.float32)
    return (entropy, masses, weighted)


def body(points, block_bucket, fine, sharp, parents, coarse_old):
    wide_count = lax.axis_size("wide")
    narrow_count = lax.axis_size("narrow")
    owner_count = wide_count * narrow_count
    block_count = block_bucket.shape[0]
    per_device = sharp.shape[0]
    feature_dim = points.shape[1]
    block_rows = points.shape[0] // block_count
    slot_total = per_device * owner_count * CAP
    positions = jnp.arange(block_count, dtype=jnp.int32)
    matching = block_bucket[:, None] == block_bucket[None, :]
    earlier = positions[None, :] < positions[:, None]
    ranking = jnp.sum(matching & earlier, axis=1)
    target = block_bucket // per_device
    local_bucket = block_bucket % per_device
    block_slot = (local_bucket * owner_count + target) * CAP + ranking
    slot_ids = jnp.arange(slot_total, dtype=jnp.int32)
    filled = slot_ids[:, None] == block_slot[None, :]
    source_block = jnp.sum(jnp.where(filled, positions[None, :], 0), axis=1)
    is_live = jnp.any(filled, axis=1)
    blocks = points.reshape(block_count, block_rows, feature_dim)
    outgoing = jnp.where(
        is_live[:, None, None], jnp.take(blocks, source_block, axis=0), jnp.zeros((), jnp.bfloat16)
    )
    outgoing = outgoing.reshape(per_device, owner_count, CAP, block_rows, feature_dim)
    live_flags = is_live.astype(jnp.int32).reshape(per_device, owner_count, CAP)
    arrived, arrived_live = (
        lax.all_to_all(outgoing, ("wide", "narrow"), split_axis=1, concat_axis=1, tiled=True),
        lax.all_to_all(live_flags, ("wide", "narrow"), split_axis=1, concat_axis=1, tiled=True),
    )
    group_coarse = coarse_old.shape[0] * narrow_count
    first_coarse = lax.axis_index("wide") * group_coarse
    bucket_size = fine.shape[0] // per_device
    local_parent = parents.reshape(per_device, bucket_size) - first_coarse
    coarse_ids = jnp.arange(group_coarse, dtype=jnp.int32)
    centroid_sets = fine.reshape(per_device, bucket_size, feature_dim)
    coarse_part = jnp.zeros((group_coarse, feature_dim), jnp.float32)
    coarse_mass = jnp.zeros((group_coarse,), jnp.float32)
    new_fine = []
    entropies = []
    for r in range(per_device):
        slot_rows = arrived[r].reshape(owner_count * CAP, block_rows, feature_dim)
        slot_live = arrived_live[r].reshape(owner_count * CAP)
        row_live = jnp.repeat(slot_live.astype(jnp.float32), block_rows)
        entropy_rows, masses, weighted = soft_assign(
            slot_rows.reshape(owner_count * CAP * block_rows, feature_dim),
            row_live,
            centroid_sets[r],
            sharp[r],
        )
        entropy_slots = entropy_rows.reshape(owner_count * CAP, block_rows)
        numerator = weighted + PRIOR_MASS * centroid_sets[r].astype(jnp.float32)
        new_fine.append((numerator / (masses + PRIOR_MASS)[:, None]).astype(jnp.bfloat16))
        entropies.append(entropy_slots)
        member = coarse_ids[:, None] == local_parent[r][None, :]
        member_matrix = member.astype(jnp.bfloat16)
        high_part = lax.optimization_barrier(numerator.astype(jnp.bfloat16))
        low_part = (numerator - high_part.astype(jnp.float32)).astype(jnp.bfloat16)
        coarse_part = (
            coarse_part
            + jnp.dot(member_matrix, high_part, preferred_element_type=jnp.float32)
            + jnp.dot(member_matrix, low_part, preferred_element_type=jnp.float32)
        )
        coarse_mass = coarse_mass + jnp.sum(
            jnp.where(member, (masses + PRIOR_MASS)[None, :], 0.0), axis=1
        )
    entropy_out = jnp.stack(entropies).reshape(per_device, owner_count, CAP, block_rows)
    returned = lax.all_to_all(
        entropy_out, ("wide", "narrow"), split_axis=1, concat_axis=1, tiled=True
    )
    point_entropy = jnp.take(returned.reshape(slot_total, block_rows), block_slot, axis=0).reshape(
        block_count * block_rows
    )
    coarse_sum, mass_sum = (
        lax.psum_scatter(
            coarse_part.astype(jnp.bfloat16), "narrow", scatter_dimension=0, tiled=True
        ).astype(jnp.float32),
        lax.psum_scatter(
            coarse_mass.astype(jnp.bfloat16), "narrow", scatter_dimension=0, tiled=True
        ).astype(jnp.float32),
    )
    coarse_new = (
        0.5 * coarse_old.astype(jnp.float32) + 0.5 * coarse_sum / (mass_sum + PRIOR_MASS)[:, None]
    ).astype(jnp.bfloat16)
    return (jnp.concatenate(new_fine, axis=0), coarse_new, point_entropy)


def solution(mesh):
    return jax.shard_map(
        body,
        mesh=mesh,
        in_specs=(
            P(("wide", "narrow"), None),
            P(("wide", "narrow")),
            P(("wide", "narrow"), None),
            P(("wide", "narrow")),
            P(("wide", "narrow")),
            P(("wide", "narrow"), None),
        ),
        out_specs=(P(("wide", "narrow"), None), P(("wide", "narrow"), None), P(("wide", "narrow"))),
        check_vma=False,
    )
```

profile of v0, /device:TPU:1, one launch (start us, length us, event | category | flops | bytes accessed | tf_op | source)
XLA Modules:
  0.0 209.1 jit_solution(2478766468083672868)
XLA Ops:
  11.5 11.5 %all-to-all-start.1 = ((s32[4,128,2]{0,2,1:T(2,128)}), s32[4,128,2]{0,2,1:T(2,128)S(1)}, u32[]{:S(2)}, u32[]{:S(2)}) async-start(s32[4,128,2]{0,2,1:T(2,128)} %copy.27), calls=%async_computation.1 | async-start | bytes 262144 | tf_op jit(solution)/shard_map/all_to_all | solution.py:58
  23.6 2.8 %reshape.230 = bf16[512,2,1024]{2,1,0:T(2,128)(2,1)S(1)} reshape(bf16[1024,1024]{1,0:T(8,128)(2,1)} %param.6) | data formatting | bytes 4194304 | tf_op jit(solution)/shard_map/reshape | solution.py:50
  26.4 15.5 %gather_fusion = bf16[1024,2,1024]{2,1,0:T(2,128)(2,1)} fusion(bf16[512,2,1024]{2,1,0:T(2,128)(2,1)S(1)} %reshape.230, s32[1024]{0:T(1024)S(1)} %broadcast_clamp_fusion), kind=kCustom, calls=%fused_computation | custom fusion | bytes 8392704 | tf_op jit(solution)/shard_map/jit(_take)/gather | solution.py:52
  41.9 7.1 %broadcast_select_fusion.1 = bf16[4,128,2,2,1024]{4,3,2,1,0:T(2,128)(2,1)S(1)} fusion(pred[4,128,2]{2,1,0:T(8,128)(4,1)S(1)} %broadcast_in_dim.123, bf16[4,128,2,2,1024]{4,3,2,1,0:T(2,128)(2,1)} %bitcast.33, pred[4,128,2]{2,1,0:T(8,128)(4,1)S(1)} %compare_and_fusion), kind=kLoop, calls=%fused_computation.3 | loop fusion | flops 4194304 | bytes 8390656 | tf_op jit(solution)/shard_map/jit(_where)/select_n | solution.py:51
  49.0 7.2 %copy.26 = bf16[4,128,2,2,1024]{4,3,2,0,1:T(2,128)(2,1)} copy(bf16[4,128,2,2,1024]{4,3,2,1,0:T(2,128)(2,1)S(1)} %broadcast_select_fusion.1) | data formatting | bytes 8388608 | tf_op jit(solution)/shard_map/jit(_where)/select_n | solution.py:51
  56.2 10.2 %all-to-all-start = ((bf16[4,128,2,2,1024]{4,3,2,0,1:T(2,128)(2,1)}), bf16[4,128,2,2,1024]{4,3,2,0,1:T(2,128)(2,1)}, u32[]{:S(2)}, u32[]{:S(2)}) async-start(bf16[4,128,2,2,1024]{4,3,2,0,1:T(2,128)(2,1)} %copy.26), calls=%async_computation | async-start | bytes 8388608 | tf_op jit(solution)/shard_map/all_to_all | solution.py:57
  69.0 3.1 %fusion = (f32[512]{0:T(512)S(1)}, f32[512]{0:T(512)S(1)}, f32[512]{0:T(512)S(1)}, f32[512]{0:T(512)S(1)}) fusion(bf16[2048,1024]{1,0:T(8,128)(2,1)} %param.8), kind=kLoop, calls=%fused_computation.13 | loop fusion | flops 6289408 | bytes 4202496 | tf_op jit(solution)/shard_map/reduce_sum | solution.py:16
  75.8 43.4 %all-to-all-done = bf16[4,128,2,2,1024]{4,3,2,0,1:T(2,128)(2,1)} async-done(((bf16[4,128,2,2,1024]{4,3,2,0,1:T(2,128)(2,1)}), bf16[4,128,2,2,1024]{4,3,2,0,1:T(2,128)(2,1)}, u32[]{:S(2)}, u32[]{:S(2)}) %all-to-all-start) | async-done | bytes 4194336 | tf_op jit(solution)/shard_map/all_to_all | solution.py:57
  119.2 6.4 %fusion.40 = (bf16[1,128,2,2,1024]{4,3,2,0,1:T(2,128)(2,1)}, bf16[1,128,2,2,1024]{4,3,2,0,1:T(2,128)(2,1)S(1)}, bf16[1,128,2,2,1024]{4,3,2,0,1:T(2,128)(2,1)S(1)}, bf16[1,128,2,2,1024]{4,3,2,0,1:T(2,128)(2,1)S(1)}) fusion(bf16[4,128,2,2,1024]{4,3,2,0,1:T(2,128)(2,1)} %all-to-all-done), kind=kLoop, calls=%fused_computation.138 | loop fusion | bytes 8388608 | tf_op jit(solution)/shard_map/slice | solution.py:71
  125.6 2.3 %reshape_reshape_squeeze.12 = bf16[512,1024]{1,0:T(8,128)(2,1)} reshape(bf16[1,128,2,2,1024]{4,3,2,0,1:T(2,128)(2,1)} %get-tuple-element.21) | data formatting | bytes 2097152 | tf_op jit(solution)/shard_map/reshape;reshape;squeeze | solution.py:75
  127.9 2.9 %fusion.50 = (f32[512]{0:T(512)S(1)}, f32[512,512]{0,1:T(8,128)S(1)}) fusion(f32[512]{0:T(512)S(1)} %get-tuple-element.60, bf16[512,1024]{1,0:T(8,128)(2,1)} %reshape_reshape_squeeze.12, bf16[2048,1024]{1,0:T(8,128)(2,1)} %param.8, f32[]{:T(128)} %bitcast), kind=kOutput, calls=%fused_computation.148 | convolution fusion | flops 537918976 | bytes 3150336 | tf_op jit(solution)/shard_map/rd,kd->rk/dot_general | solution.py:14
  134.2 3.0 %fusion.49 = (f32[512]{0:T(512)S(1)}, f32[512,512]{0,1:T(8,128)S(1)}) fusion(f32[512]{0:T(512)S(1)} %get-tuple-element.59, bf16[512,1024]{1,0:T(8,128)(2,1)} %reshape_reshape_squeeze.13, bf16[2048,1024]{1,0:T(8,128)(2,1)} %param.8, f32[]{:T(128)} %bitcast.4), kind=kOutput, calls=%fused_computation.147 | convolution fusion | flops 537918976 | bytes 3150336 | tf_op jit(solution)/shard_map/rd,kd->rk/dot_general | solution.py:14
  139.7 2.5 %fusion.48 = (f32[512]{0:T(512)S(1)}, f32[512,512]{0,1:T(8,128)S(1)}) fusion(f32[512]{0:T(512)S(1)} %get-tuple-element.58, bf16[512,1024]{1,0:T(8,128)(2,1)S(1)} %reshape_reshape_squeeze.14, bf16[2048,1024]{1,0:T(8,128)(2,1)} %param.8, f32[]{:T(128)} %bitcast.5), kind=kOutput, calls=%fused_computation.146 | convolution fusion | flops 537918976 | bytes 3150336 | tf_op jit(solution)/shard_map/rd,kd->rk/dot_general | solution.py:14
  145.1 2.6 %fusion.47 = (f32[512]{0:T(512)S(1)}, f32[512,512]{0,1:T(8,128)S(1)}) fusion(f32[512]{0:T(512)} %get-tuple-element.57, bf16[512,1024]{1,0:T(8,128)(2,1)S(1)} %reshape_reshape_squeeze.15, bf16[2048,1024]{1,0:T(8,128)(2,1)} %param.8, f32[]{:T(128)} %bitcast.6), kind=kOutput, calls=%fused_computation.145 | convolution fusion | flops 537918976 | bytes 3150336 | tf_op jit(solution)/shard_map/rd,kd->rk/dot_general | solution.py:14
  149.6 2.3 %copy.28 = f32[4,128,2,2]{0,3,2,1:T(2,128)} copy(f32[4,128,2,2]{3,2,1,0:T(2,128)S(1)} %pad_maximum_fusion.1) | data formatting | bytes 16384 | tf_op jit(solution)/shard_map/stack | solution.py:96
  151.9 4.2 %all-to-all-start.2 = ((f32[4,128,2,2]{0,3,2,1:T(2,128)}), f32[4,128,2,2]{0,3,2,1:T(2,128)S(1)}, u32[]{:S(2)}, u32[]{:S(2)}) async-start(f32[4,128,2,2]{0,3,2,1:T(2,128)} %copy.28), calls=%async_computation.3 | async-start | bytes 524288 | tf_op jit(solution)/shard_map/all_to_all | solution.py:97
  156.4 3.3 %fusion.44 = (bf16[512,1024]{1,0:T(8,128)(2,1)S(1)}, bf16[512,1024]{1,0:T(8,128)(2,1)}, f32[512,1024]{1,0:T(8,128)S(1)}) fusion(f32[512]{0:T(512)S(1)} %broadcast_add_fusion.3, bf16[2048,1024]{1,0:T(8,128)(2,1)} %param.8, bf16[512,512]{0,1:T(8,128)(2,1)} %get-tuple-element.14, bf16[512,1024]{1,0:T(8,128)(2,1)S(1)} %copy-done.1), kind=kOutput, calls=%fused_computation.142 | convolution fusion | flops 539492352 | bytes 6817792 | tf_op jit(solution)/shard_map/rk,rd->kd/dot_general | solution.py:26
  161.0 1.8 fusion.43
  163.0 1.8 fusion.42
  164.8 1.8 fusion.41
  170.9 13.0 %all-reduce = bf16[256]{0:T(256)(128)(2,1)S(1)} all-reduce(bf16[256]{0:T(256)(128)(2,1)S(1)} %add_convert_fusion.1), channel_id=3, replica_groups=mesh['wide'=16,'narrow'=8] {'narrow'}, use_global_device_ids=true, to_apply=%region_24.25.clone | all-reduce | flops 256 | bytes 1024
  183.9 7.8 %pad_maximum_fusion = bf16[2048,1024]{1,0:T(8,128)(2,1)} fusion(bf16[512,1024]{1,0:T(8,128)(2,1)} %get-tuple-element.26, bf16[512,1024]{1,0:T(8,128)(2,1)} %get-tuple-element.28, bf16[512,1024]{1,0:T(8,128)(2,1)S(1)} %copy-done.6, bf16[512,1024]{1,0:T(8,128)(2,1)S(1)} %copy-done.5), kind=kLoop, calls=%fused_computation.4 | loop fusion | flops 16777216 | bytes 8388608 | tf_op jit(solution)/shard_map/concatenate | solution.py:114
  191.7 2.0 copy.29
  195.6 5.1 %reduce-scatter.2.cloned.1.call-done = bf16[32,1024]{1,0:T(8,128)(2,1)} async-done(((bf16[256,1024]{1,0:T(8,128)(2,1)}), bf16[32,1024]{1,0:T(8,128)(2,1)}) %reduce-scatter.2.cloned.1.call-update) | async-done | bytes 65552 | tf_op jit(solution)/shard_map/reduce_scatter | solution.py:104
  (118 shorter events, 30.6 us)
Async XLA Ops:
  11.5 44.7 %all-to-all-start.1 = ((s32[4,128,2]{0,2,1:T(2,128)}), s32[4,128,2]{0,2,1:T(2,128)S(1)}, u32[]{:S(2)}, u32[]{:S(2)}) async-start(s32[4,128,2]{0,2,1:T(2,128)} %copy.27), calls=%async_computation.1 | async-start | bytes 262144 | tf_op jit(solution)/shard_map/all_to_all | solution.py:58
  56.2 10.3 %copy-start.19 = (u32[128]{0:T(128)S(1)}, u32[128]{0:T(128)}, u32[]{:S(2)}) copy-start(u32[128]{0:T(128)} %constant.90) | copy-start | bytes 1540
  56.2 12.1 %copy-start.17 = (f32[4]{0:T(128)S(1)}, f32[4]{0:T(128)}, u32[]{:S(2)}) copy-start(f32[4]{0:T(128)} %param.9) | copy-start | bytes 52
  56.2 63.0 %all-to-all-start = ((bf16[4,128,2,2,1024]{4,3,2,0,1:T(2,128)(2,1)}), bf16[4,128,2,2,1024]{4,3,2,0,1:T(2,128)(2,1)}, u32[]{:S(2)}, u32[]{:S(2)}) async-start(bf16[4,128,2,2,1024]{4,3,2,0,1:T(2,128)(2,1)} %copy.26), calls=%async_computation | async-start | bytes 8388608 | tf_op jit(solution)/shard_map/all_to_all | solution.py:57
  69.0 3.7 %copy-start.16 = (s32[2048]{0:T(1024)S(1)}, s32[2048]{0:T(1024)}, u32[]{:S(2)}) copy-start(s32[2048]{0:T(1024)} %param.10) | copy-start | bytes 24580
  145.1 2.6 %copy-start.3 = (bf16[512,1024]{1,0:T(8,128)(2,1)}, bf16[512,1024]{1,0:T(8,128)(2,1)S(1)}, u32[]{:S(2)}) copy-start(bf16[512,1024]{1,0:T(8,128)(2,1)S(1)} %reshape_reshape_squeeze.15) | copy-start | bytes 3145732
  145.1 2.8 %copy-start.12 = (f32[512]{0:T(512)S(1)}, f32[512]{0:T(512)}, u32[]{:S(2)}) copy-start(f32[512]{0:T(512)} %mul.183) | copy-start | bytes 6148
  147.9 8.3 %copy-start.13 = (f32[512]{0:T(512)S(1)}, f32[512]{0:T(512)}, u32[]{:S(2)}) copy-start(f32[512]{0:T(512)} %get-tuple-element.13) | copy-start | bytes 6148
  147.9 8.3 %copy-start.14 = (f32[512]{0:T(512)S(1)}, f32[512]{0:T(512)}, u32[]{:S(2)}) copy-start(f32[512]{0:T(512)} %get-tuple-element.15) | copy-start | bytes 6148
  147.9 8.3 %copy-start.15 = (f32[512]{0:T(512)S(1)}, f32[512]{0:T(512)}, u32[]{:S(2)}) copy-start(f32[512]{0:T(512)} %get-tuple-element.17) | copy-start | bytes 6148
  147.9 8.4 %copy-start.1 = (bf16[512,1024]{1,0:T(8,128)(2,1)S(1)}, bf16[512,1024]{1,0:T(8,128)(2,1)}, u32[]{:S(2)}) copy-start(bf16[512,1024]{1,0:T(8,128)(2,1)} %reshape_reshape_squeeze.12) | copy-start | bytes 3145732
  151.9 39.8 %all-to-all-start.2 = ((f32[4,128,2,2]{0,3,2,1:T(2,128)}), f32[4,128,2,2]{0,3,2,1:T(2,128)S(1)}, u32[]{:S(2)}, u32[]{:S(2)}) async-start(f32[4,128,2,2]{0,3,2,1:T(2,128)} %copy.28), calls=%async_computation.3 | async-start | bytes 524288 | tf_op jit(solution)/shard_map/all_to_all | solution.py:97
  156.1 44.6 %reduce-scatter.2.cloned.1.call-start = ((), (), s32[]{:S(2)}) async-start(), calls=%async_computation.4 | async-start | bytes 589824 | tf_op jit(solution)/shard_map/reduce_scatter | solution.py:104
  156.4 3.9 %copy-start = (bf16[2048,1024]{1,0:T(8,128)(2,1)S(1)}, bf16[2048,1024]{1,0:T(8,128)(2,1)}, u32[]{:S(2)}) copy-start(bf16[2048,1024]{1,0:T(8,128)(2,1)} %param.8) | copy-start | bytes 12582916
  159.7 1.2 copy-start.2
  159.7 1.4 copy-start.7
  161.0 1.9 copy-start.8
  163.0 1.8 copy-start.4
  163.0 1.8 copy-start.9
  169.4 14.5 %copy-start.5 = (bf16[512,1024]{1,0:T(8,128)(2,1)S(1)}, bf16[512,1024]{1,0:T(8,128)(2,1)}, u32[]{:S(2)}) copy-start(bf16[512,1024]{1,0:T(8,128)(2,1)} %get-tuple-element.32) | copy-start | bytes 3145732
  169.4 14.5 %copy-start.6 = (bf16[512,1024]{1,0:T(8,128)(2,1)S(1)}, bf16[512,1024]{1,0:T(8,128)(2,1)}, u32[]{:S(2)}) copy-start(bf16[512,1024]{1,0:T(8,128)(2,1)} %get-tuple-element.30) | copy-start | bytes 3145732
  183.9 9.8 %copy-start.11 = (s32[1024]{0:T(1024)S(1)}, s32[1024]{0:T(1024)}, u32[]{:S(2)}) copy-start(s32[1024]{0:T(1024)} %pad_clamp_fusion) | copy-start | bytes 12292
  191.6 3.1 %copy-start.18 = (pred[512]{0:T(512)(128)(4,1)S(1)}, pred[512]{0:T(512)(128)(4,1)}, u32[]{:S(2)}) copy-start(pred[512]{0:T(512)(128)(4,1)} %get-tuple-element.11) | copy-start | bytes 1540
  191.6 9.1 %copy-start.10 = (bf16[32,1024]{1,0:T(8,128)(2,1)S(1)}, bf16[32,1024]{1,0:T(8,128)(2,1)}, u32[]{:S(2)}) copy-start(bf16[32,1024]{1,0:T(8,128)(2,1)} %param.11) | copy-start | bytes 196612
Sparse Core Ops, SparseCore 0:
  170.8 29.8 reduce-scatter.1
where the time goes:
time: 212 us; the launch traced here: 209 us
  local copies, waits for them, and re-layouts  49.5 us (23%)
  waiting for transfers between devices  48.5 us (23%)
  other arithmetic  32.7 us (15%)
  starting transfers between devices  26 us (12%)
  matrix products  24.2 us (11%)
  between operations  15.2 us (7%)
  blocking collectives  13 us (6%)
    all_to_all x1, waiting for transfers between devices, body(): lax.all_to_all(outgoing, ('wide', 'narrow'), split_axis=1, concat_axis=1,...  43.4 us
    gather x1, local copies, waits for them, and re-layouts, body(): jnp.take(blocks, source_block, axis=0)  15.5 us
    unnamed x1, blocking collectives  13 us
    all_to_all x1, starting transfers between devices, body(): lax.all_to_all(live_flags, ('wide', 'narrow'), split_axis=1, concat_axis=...  11.5 us
    dot_general x4, matrix products, soft_assign(): jnp.einsum('rd,kd->rk', row_data, centroids, preferred_element_type=jnp.f...  11 us
    all_to_all x1, starting transfers between devices, body(): lax.all_to_all(outgoing, ('wide', 'narrow'), split_axis=1, concat_axis=1,...  10.2 us
    dot_general x4, matrix products, soft_assign(): jnp.einsum('rk,rd->kd', weights, row_data, preferred_element_type=jnp.flo...  8.62 us
    concatenate x1, other arithmetic, body(): return (jnp.concatenate(new_fine, axis=0), coarse_new, point_entropy)  7.75 us
  transfers between devices with their start and end apart: 4, of which 2 were waited for; matrix products, arithmetic and copies ran while one was open for 32% of the time, Pallas kernels for 0%

commit v1 on v0

v1 whole, which is shorter than its diff:
```python
import functools

import jax
import jax.numpy as jnp
from jax import lax
from jax.experimental import pallas as pl
from jax.experimental.pallas import tpu as pltpu
from jax.sharding import PartitionSpec as P

MESH = pl.DeviceIdType.MESH
F32 = jnp.float32
BF16 = jnp.bfloat16

CAP = 2
PRIOR_MASS = 1.0
STRIDE = 37
DEAD_MARK = 16.0
EXTRA = 16


def iota(shape, axis):
    return lax.broadcasted_iota(jnp.int32, shape, axis)


def dot(a, b, ca=1, cb=0):
    return lax.dot_general(a, b, (((ca,), (cb,)), ((), ())), preferred_element_type=F32)


def split(value):
    high = value.astype(BF16)
    return high, (value - high.astype(F32)).astype(BF16)


def kernel(
    dims,
    sharp_ref,
    bucket_ref,
    parent_hbm,
    points_hbm,
    fine_hbm,
    old_hbm,
    fine_out,
    coarse_out,
    entropy_out,
    points,
    cent,
    half_norm,
    parent,
    old,
    code,
    place,
    src,
    dst,
    numer,
    mass,
    staged,
    coarse,
    coarse_mass,
    ent,
    ret,
    core_send,
    core_recv,
    y_send,
    y_recv,
    load_sem,
    cent_sem,
    send_sem,
    recv_sem,
    ent_send_sem,
    ent_recv_sem,
    out_sem,
    core_sem,
    y_send_sem,
    y_recv_sem,
):
    wide, narrow = dims
    owners = wide * narrow
    buckets, _, block_slots, width = src.shape
    slot_rows = owners * block_slots
    size = half_norm.shape[1]
    n_points = points.shape[0]
    group = coarse.shape[0]
    inverse = pow(STRIDE, -1, owners)
    w, n = lax.axis_index("wide"), lax.axis_index("narrow")
    me = w * narrow + n

    def device(i):
        t = lax.rem(me + STRIDE * i, owners)
        return (t // narrow, lax.rem(t, narrow))

    def source(i):
        t = lax.rem(me + (owners - STRIDE) * i, owners)
        return (t // narrow, lax.rem(t, narrow))

    points_copy = pltpu.make_async_copy(points_hbm, points, load_sem.at[0])
    points_copy.start()
    barrier = pltpu.get_barrier_semaphore()

    @pl.loop(1, owners)
    def _(i):
        pl.semaphore_signal(barrier, inc=1, device_id=device(i), device_id_type=MESH)

    parent_copy = pltpu.make_async_copy(parent_hbm, parent, load_sem.at[1])
    parent_copy.start()
    old_copy = pltpu.make_async_copy(old_hbm, old, load_sem.at[2])
    old_copy.start()
    cent_copies = [
        pltpu.make_async_copy(
            fine_hbm.at[pl.ds(r * size, size)], cent.at[r, pl.ds(0, size)], cent_sem.at[r]
        )
        for r in range(buckets)
    ]
    for copy in cent_copies:
        copy.start()

    n_blocks = bucket_ref.shape[1]
    per_tile = 128 // 2
    column = jnp.transpose(jnp.broadcast_to(bucket_ref[...].astype(F32), (128, n_blocks)))
    lane = iota((1, 128), 1)
    for j in range(n_points // 128):
        own = column[per_tile * j : per_tile * (j + 1)]
        pick = iota((per_tile, 128), 0) == iota((per_tile, 128), 1) // 2
        name = jnp.sum(jnp.where(pick, own, 0.0), axis=0, keepdims=True)
        earlier = iota((n_blocks, 128), 0) < per_tile * j + iota((n_blocks, 128), 1) // 2
        rank = jnp.sum(jnp.where((column == name) & earlier, 1.0, 0.0), axis=0, keepdims=True)
        number = name.astype(jnp.int32)
        step = ((number // buckets - me) * inverse) & (owners - 1)
        tile = pl.ds(128 * j, 128)
        place[:, tile] = step
        code[:, tile] = (
            (number % buckets) * slot_rows
            + step * block_slots
            + rank.astype(jnp.int32) * (block_slots // CAP)
            + (lane & 1)
        )

    points_copy.wait()

    part = 256
    steps_in_part = part // block_slots

    def gather_part(r, c):
        base = r * slot_rows + c * part
        mask = code[...] - base == iota((part, n_points), 0)
        hot = jnp.where(mask, 1.0, 0.0)
        live = jnp.sum(hot, axis=1, keepdims=True)
        rows = dot(hot.astype(BF16), points[...])
        mark = jnp.where((iota((part, 128), 1) == 0) & (live < 0.5), DEAD_MARK, rows[:, :128])
        rows = jnp.concatenate([mark, rows[:, 128:]], axis=1).astype(BF16)
        src[r, pl.ds(c * steps_in_part, steps_in_part)] = rows.reshape(
            steps_in_part, block_slots, width
        )

    quarter = owners // 4

    def send_part(r, c):
        first = c * steps_in_part

        @pl.loop(first, first + steps_in_part)
        def _(i):
            @pl.when(i > 0)
            def _():
                pltpu.make_async_remote_copy(
                    src_ref=src.at[r, i],
                    dst_ref=dst.at[r, i],
                    send_sem=send_sem.at[r],
                    recv_sem=recv_sem.at[r, i // quarter],
                    device_id=device(i),
                    device_id_type=MESH,
                ).start()

    def send_own(r):
        pltpu.make_async_copy(src.at[r, 0], dst.at[r, 0], recv_sem.at[r, 0]).start()

    parts = slot_rows // part

    def send_bucket(r):
        @pl.loop(0, parts)
        def _(c):
            gather_part(r, c)
            send_part(r, c)

        send_own(r)

    def prepare(r):
        cent_copies[r].wait()
        corner = (iota((EXTRA, width), 0) == 0) & (iota((EXTRA, width), 1) == 0)
        cent[r, pl.ds(size, EXTRA)] = jnp.where(corner, 1.0, 0.0).astype(BF16)

        @pl.loop(0, size // 64)
        def _(b):
            rows = pl.ds(pl.multiple_of(b * 64, 64), 64)
            value = cent[r, rows].astype(F32)
            norm = jnp.sum(value * value, axis=1, keepdims=True)
            half_norm[r, rows] = jnp.broadcast_to(0.5 * norm, (64, 128))

    def assign(r, first, steps):
        rows = steps * block_slots
        for q in range(first // quarter, (first + steps) // quarter):
            landed = dst.at[r, pl.ds(q * quarter, quarter)]
            pltpu.make_async_copy(landed, landed, recv_sem.at[r, q]).wait()
        x = dst[r, pl.ds(first, steps)].reshape(rows, width)
        products = dot(cent[r], x, 1, 1)
        live = jnp.where(products[size : size + 1] < 0.75 * DEAD_MARK, 1.0, 0.0)
        norm = jnp.concatenate([half_norm[r]] * (rows // 128), axis=1)
        logits = (products[:size] - norm) * (sharp_ref[r] * width**-0.5)
        shifted = logits - jnp.max(logits, axis=0, keepdims=True)
        exponent = jnp.exp(shifted)
        total = jnp.sum(exponent, axis=0, keepdims=True)
        inverse_total = 1.0 / total
        entropy = jnp.log(total) - jnp.sum(exponent * shifted, axis=0, keepdims=True) * inverse_total
        for q in range(rows // 128):
            ent[r, first // quarter + q] = entropy[:, 128 * q : 128 * (q + 1)]

        @pl.loop(first, first + steps)
        def _(i):
            @pl.when(i > 0)
            def _():
                pltpu.make_async_remote_copy(
                    src_ref=ent.at[r, i // quarter],
                    dst_ref=ret.at[r, i],
                    send_sem=ent_send_sem.at[r],
                    recv_sem=ent_recv_sem.at[r],
                    device_id=source(i),
                    device_id_type=MESH,
                ).start()

        if first == 0:
            pltpu.make_async_copy(ent.at[r, 0], ret.at[r, 0], ent_recv_sem.at[r]).start()

        weights = (exponent * (inverse_total * live)).astype(BF16)
        weighed = dot(weights, jnp.ones((rows, 128), BF16))
        weighted = dot(weights, x)
        if first == 0:
            mass[...] = weighed + PRIOR_MASS
            numer[...] = weighted + PRIOR_MASS * cent[r, pl.ds(0, size)].astype(F32)
        else:
            mass[...] += weighed
            numer[...] += weighted

    def finish(r):
        own = parent[:, pl.ds(r * size, size)] - w * group
        member = jnp.where(own == iota((group, size), 0), 1.0, 0.0).astype(BF16)
        high, low = split(mass[...])
        part_mass = dot(member, high) + dot(member, low)
        part_sum = dot(member, numer[...].astype(BF16))
        if r == 0:
            coarse_mass[...] = part_mass
            coarse[...] = part_sum
        else:
            coarse_mass[...] += part_mass
            coarse[...] += part_sum

    def emit(r):
        if r >= 2:
            out_copy(r - 2).wait()
        scale = 1.0 / mass[...]
        for d in range(width // 128):
            cols = pl.ds(128 * d, 128)
            staged[r % 2, :, cols] = (numer[:, cols] * scale).astype(BF16)
        out_copy(r).start()

    def out_copy(r):
        return pltpu.make_async_copy(
            staged.at[r % 2], fine_out.at[pl.ds(r * size, size)], out_sem.at[r % 2]
        )

    def collect(r):
        pltpu.make_async_copy(ret.at[r], ret.at[r], ent_recv_sem.at[r]).wait()
        high, low = split(ret[r].reshape(owners, 128))
        hot = jnp.where(place[...] == iota((owners, n_points), 0), 1.0, 0.0).astype(BF16)
        found = dot(high, hot, 0, 0) + dot(low, hot, 0, 0)
        mine = (code[...] & 127) == iota((128, n_points), 0)
        mine = mine & (code[...] // slot_rows == r)
        value = jnp.sum(jnp.where(mine, found, 0.0), axis=0, keepdims=True)
        if r == 0:
            entropy_out[...] = value
        else:
            entropy_out[...] += value

    def whole_bucket(r):
        half = owners // 2
        assign(r, 0, half)
        assign(r, half, half)
        finish(r)
        emit(r)

    @pl.loop(0, parts)
    def _(c):
        gather_part(0, c)

    pl.semaphore_wait(barrier, owners - 1)

    @pl.loop(0, parts)
    def _(c):
        send_part(0, c)

    send_own(0)
    send_bucket(1)
    parent_copy.wait()
    prepare(0)
    send_bucket(2)
    whole_bucket(0)
    send_bucket(3)
    prepare(1)
    whole_bucket(1)
    collect(0)
    prepare(2)
    whole_bucket(2)
    collect(1)
    prepare(3)
    collect(2)
    for q in range(4):
        assign(3, q * quarter, quarter)
    finish(3)

    y, core = n // 2, lax.rem(n, 2)
    ys = narrow // 2
    own_rows = group // narrow

    def tile_of(value):
        high, low = split(value)
        return jnp.where(iota((own_rows, 128), 1) < 64, high.astype(F32), low.astype(F32))

    def whole_of(value):
        return value + pltpu.roll(value, 64, 1)

    for k in range(ys):
        rows = pl.ds(pl.multiple_of((2 * k + 1 - core) * own_rows, own_rows), own_rows)
        core_send[k, :, pl.ds(0, width)] = coarse[rows].astype(BF16)
        core_send[k, :, pl.ds(width, 128)] = tile_of(coarse_mass[rows]).astype(BF16)
    core_copy = pltpu.make_async_remote_copy(
        src_ref=core_send,
        dst_ref=core_recv,
        send_sem=core_sem.at[0],
        recv_sem=core_sem.at[1],
        device_id=(w, n + 1 - 2 * core),
        device_id_type=MESH,
    )
    core_copy.start()
    emit(3)
    core_copy.wait()

    def chip_sum(k):
        rows = pl.ds(pl.multiple_of((2 * k + core) * own_rows, own_rows), own_rows)
        total = coarse[rows] + core_recv[k, :, pl.ds(0, width)].astype(F32)
        weight = coarse_mass[rows] + whole_of(core_recv[k, :, pl.ds(width, 128)].astype(F32))
        return total, weight

    y_copies = []
    for k in range(1, ys):
        other = lax.rem(y + k, ys)
        total, weight = chip_sum(other)
        y_send[k - 1, :, pl.ds(0, width)] = total.astype(BF16)
        y_send[k - 1, :, pl.ds(width, 128)] = tile_of(weight).astype(BF16)
        copy = pltpu.make_async_remote_copy(
            src_ref=y_send.at[k - 1],
            dst_ref=y_recv.at[k - 1],
            send_sem=y_send_sem.at[k - 1],
            recv_sem=y_recv_sem.at[k - 1],
            device_id=(w, 2 * other + core),
            device_id_type=MESH,
        )
        copy.start()
        y_copies.append(copy)
    total, weight = chip_sum(y)
    old_copy.wait()
    collect(3)
    for k, copy in enumerate(y_copies):
        copy.wait()
        total = total + y_recv[k, :, pl.ds(0, width)].astype(F32)
        weight = weight + whole_of(y_recv[k, :, pl.ds(width, 128)].astype(F32))
    scale = 0.5 / (weight + PRIOR_MASS)
    for d in range(width // 128):
        cols = pl.ds(128 * d, 128)
        here = total[:, 128 * d : 128 * (d + 1)]
        coarse_out[:, cols] = (0.5 * old[:, cols].astype(F32) + here * scale).astype(BF16)

    for r in range(buckets):
        sent = src.at[r, pl.ds(0, owners - 1)]
        pltpu.make_async_copy(sent, sent, send_sem.at[r]).wait()
        sent = ret.at[r, pl.ds(0, owners - 1)]
        pltpu.make_async_copy(sent, sent, ent_send_sem.at[r]).wait()
    out_copy(2).wait()
    out_copy(3).wait()


def body(points, block_bucket, fine, sharp, parents, coarse_old):
    wide, narrow = lax.axis_size("wide"), lax.axis_size("narrow")
    owners = wide * narrow
    n_points, width = points.shape
    n_blocks = block_bucket.shape[0]
    buckets = sharp.shape[0]
    size = fine.shape[0] // buckets
    block_slots = CAP * (n_points // n_blocks)
    own_rows = coarse_old.shape[0]
    group = own_rows * narrow
    ys = narrow // 2
    whole = pl.BlockSpec(memory_space=pltpu.VMEM)
    anywhere = pl.BlockSpec(memory_space=pl.ANY)
    dma = pltpu.SemaphoreType.DMA
    fine_new, coarse_new, entropy = pl.pallas_call(
        functools.partial(kernel, (wide, narrow)),
        out_shape=(
            jax.ShapeDtypeStruct(fine.shape, BF16),
            jax.ShapeDtypeStruct(coarse_old.shape, BF16),
            jax.ShapeDtypeStruct((1, n_points), F32),
        ),
        in_specs=[pl.BlockSpec(memory_space=pltpu.SMEM), whole] + [anywhere] * 4,
        out_specs=(anywhere, whole, whole),
        scratch_shapes=[
            pltpu.VMEM((n_points, width), BF16),
            pltpu.VMEM((buckets, size + EXTRA, width), BF16),
            pltpu.VMEM((buckets, size, 128), F32),
            pltpu.VMEM((1, buckets * size), jnp.int32),
            pltpu.VMEM((own_rows, width), BF16),
            pltpu.VMEM((1, n_points), jnp.int32),
            pltpu.VMEM((1, n_points), jnp.int32),
            pltpu.VMEM((buckets, owners, block_slots, width), BF16),
            pltpu.VMEM((buckets, owners, block_slots, width), BF16),
            pltpu.VMEM((size, width), F32),
            pltpu.VMEM((size, 128), F32),
            pltpu.VMEM((2, size, width), BF16),
            pltpu.VMEM((group, width), F32),
            pltpu.VMEM((group, 128), F32),
            pltpu.VMEM((buckets, 4, 1, 128), F32),
            pltpu.VMEM((buckets, owners, 1, 128), F32),
            pltpu.VMEM((ys, own_rows, width + 128), BF16),
            pltpu.VMEM((ys, own_rows, width + 128), BF16),
            pltpu.VMEM((ys - 1, own_rows, width + 128), BF16),
            pltpu.VMEM((ys - 1, own_rows, width + 128), BF16),
            dma((3,)),
            dma((buckets,)),
            dma((buckets,)),
            dma((buckets, 4)),
            dma((buckets,)),
            dma((buckets,)),
            dma((2,)),
            dma((2,)),
            dma((ys - 1,)),
            dma((ys - 1,)),
        ],
        compiler_params=pltpu.CompilerParams(
            collective_id=0, has_side_effects=True, vmem_limit_bytes=56 << 20
        ),
    )(
        sharp,
        block_bucket.reshape(1, n_blocks),
        parents.reshape(1, buckets * size),
        points,
        fine,
        coarse_old,
    )
    return fine_new, coarse_new, entropy.reshape(n_points)


def solution(mesh):
    both = ("wide", "narrow")
    return jax.shard_map(
        body,
        mesh=mesh,
        in_specs=(P(both, None), P(both), P(both, None), P(both), P(both), P(both, None)),
        out_specs=(P(both, None), P(both, None), P(both)),
        check_vma=False,
    )
```

time: 212 us -> 90.8 us (0.43); the launches traced: 209 us -> 90.6 us
  Pallas kernels: 0 us -> 84.1 us
  waiting for transfers between devices: 48.5 us -> 0 us
  local copies, waits for them, and re-layouts: 49.5 us -> 5.9 us
  other arithmetic: 32.7 us -> 0 us
  starting transfers between devices: 26 us -> 0 us
  matrix products: 24.2 us -> 0 us
  between operations: 15.2 us -> 0.66 us
  blocking collectives: 13 us -> 0 us
    pallas_call x0 -> x1, Pallas kernels: none -> 84.1 us  [body(): pl.pallas_call(functools.partial(kernel, (wide, narrow)), out_shape=(jax....]
    all_to_all x3 -> x0, waiting for transfers between devices: 43.4 us -> none  [the longest x1 43.4 us: body(): lax.all_to_all(outgoing, ('wide', 'narrow'), split_axis=1, concat_axis=1,...]
    all_to_all x3 -> x0, starting transfers between devices: 25.9 us -> none  [the longest x1 11.5 us: body(): lax.all_to_all(live_flags, ('wide', 'narrow'), split_axis=1, concat_axis=...]
    dot_general x16 -> x0, matrix products: 24.2 us -> none  [the longest x4 11 us: soft_assign(): jnp.einsum('rd,kd->rk', row_data, centroids, preferred_element_type=jnp.f...]
    gather x2 -> x0, local copies, waits for them, and re-layouts: 16.5 us -> none  [the longest x1 15.5 us: body(): jnp.take(blocks, source_block, axis=0)]
    unnamed x1 -> x0, blocking collectives: 13 us -> none
    reduce_sum x15 -> x0, other arithmetic: 11.8 us -> none  [the longest x4 6.15 us: soft_assign(): masses = jnp.sum(weights.astype(jnp.float32), axis=0)]
    select_n x2 -> x0, local copies, waits for them, and re-layouts: 7.94 us -> none  [the longest x1 7.18 us: body(): jnp.where(is_live[:, None, None], jnp.take(blocks, source_block, axis=0),...]
  transfers between devices with their start and end apart: 4 -> 0, of which waited for: 2 -> 0; matrix products, arithmetic and copies ran while one was open for 32% -> 0% of each run, Pallas kernels for 0% -> 0%
where the time goes in v1:
time: 90.8 us; the launch traced here: 90.6 us
  Pallas kernels  84.1 us (93%)
  local copies, waits for them, and re-layouts  5.9 us (6%)
    pallas_call x1, Pallas kernels, body(): pl.pallas_call(functools.partial(kernel, (wide, narrow)), out_shape=(jax....  84.1 us
    unnamed x7, local copies, waits for them, and re-layouts  5.9 us

profile of v1, /device:TPU:1, one launch (start us, length us, event | category | flops | bytes accessed | tf_op | source)
XLA Modules:
  0.0 90.6 jit_solution(14773624458008670926)
XLA Ops:
  0.6 84.1 %shard_map.85 = (bf16[2048,1024]{1,0:T(8,128)(2,1)}, bf16[32,1024]{1,0:T(8,128)(2,1)}, f32[1,1024]{1,0:T(1,128)}) custom-call(f32[4]{0:T(128)} %sharp_ref.1, s32[1,512]{1,0:T(1,128)} %bitcast.5, s32[1,2048]{1,0:T(1,128)} %bitcast.3, bf16[1024,1024]{1,0:T(8,128)(2,1)} %points_hbm.1, bf16[2048,1024]{1,0:T(8,128)(2,1)} %fine_hbm.1, bf16[32,1024]{1,0:T(8,128)(2,1)} %old_hbm.1), custom_call_target="tpu_custom_call" | custom-call | tf_op jit(solution)/shard_map/pallas_call | solution.py:402
  84.7 0.0 copy-start
  84.7 0.0 copy-start.1
  84.7 4.7 %copy.12 = bf16[2048,1024]{1,0:T(8,128)(2,1)} copy(bf16[2048,1024]{1,0:T(8,128)(2,1)} %get-tuple-element.12) | data formatting | bytes 8388608
  89.4 0.0 copy-done
  89.4 0.6 copy.13
  90.0 0.0 copy-done.1
  90.0 0.6 copy.14
Async XLA Ops:
  84.7 4.7 %copy-start = (bf16[32,1024]{1,0:T(8,128)(2,1)S(1)}, bf16[32,1024]{1,0:T(8,128)(2,1)}, u32[]{:S(2)}) copy-start(bf16[32,1024]{1,0:T(8,128)(2,1)} %get-tuple-element.13) | copy-start | bytes 196612
  84.7 5.3 %copy-start.1 = (f32[1,1024]{1,0:T(1,128)S(1)}, f32[1,1024]{1,0:T(1,128)}, u32[]{:S(2)}) copy-start(f32[1,1024]{1,0:T(1,128)} %get-tuple-element.8) | copy-start | bytes 12292

commit v2 on v1

v2 whole, which is shorter than its diff:
```python
import functools

import jax
import jax.numpy as jnp
from jax import lax
from jax.experimental import pallas as pl
from jax.experimental.pallas import tpu as pltpu
from jax.sharding import PartitionSpec as P

MESH = pl.DeviceIdType.MESH
F32 = jnp.float32
BF16 = jnp.bfloat16

CAP = 2
PRIOR_MASS = 1.0
STRIDE = 37
DEAD_MARK = 16.0
EXTRA = 16


def iota(shape, axis):
    return lax.broadcasted_iota(jnp.int32, shape, axis)


def dot(a, b, ca=1, cb=0):
    return lax.dot_general(a, b, (((ca,), (cb,)), ((), ())), preferred_element_type=F32)


def split(value):
    high = value.astype(BF16)
    return high, (value - high.astype(F32)).astype(BF16)


def collect(found_in, code, place, mine_of):
    owners, n_points = found_in.shape[0], code.shape[1]
    high, low = split(found_in)
    hot = jnp.where(place == iota((owners, n_points), 0), 1.0, 0.0).astype(BF16)
    found = dot(high, hot, 0, 0) + dot(low, hot, 0, 0)
    mine = mine_of(iota((128, n_points), 0))
    return jnp.sum(jnp.where(mine, found, 0.0), axis=0, keepdims=True)


def kernel(
    dims,
    sharp_ref,
    bucket_ref,
    parent_hbm,
    points_hbm,
    fine_hbm,
    old_hbm,
    fine_out,
    coarse_out,
    entropy_out,
    code,
    back_out,
    points,
    cent,
    half_norm,
    parent,
    old,
    src,
    dst,
    numer,
    mass,
    coarse,
    coarse_mass,
    packed,
    packed_back,
    ent,
    back,
    core_send0,
    core_send1,
    core_recv0,
    core_recv1,
    y_send0,
    y_send1,
    y_recv0,
    y_recv1,
    load_sem,
    cent_sem,
    send_sem,
    recv_sem,
    ent_send_sem,
    ent_recv_sem,
    core_send_sem,
    core_recv_sem,
    y_send_sem,
    y_recv_sem,
):
    wide, narrow = dims
    owners = wide * narrow
    buckets, _, block_slots, width = src.shape
    slot_rows = owners * block_slots
    size = half_norm.shape[1]
    n_points = points.shape[0]
    group = coarse.shape[0]
    inverse = pow(STRIDE, -1, owners)
    quarter = owners // 4
    last = buckets - 1
    w, n = lax.axis_index("wide"), lax.axis_index("narrow")
    me = w * narrow + n

    def device(i):
        t = lax.rem(me + STRIDE * i, owners)
        return (lax.div(t, narrow), lax.rem(t, narrow))

    def source(i):
        t = lax.rem(me + (owners - STRIDE) * i, owners)
        return (lax.div(t, narrow), lax.rem(t, narrow))

    def each_step(first, stop, act):
        if first == 0:
            for i in range(1, 4):
                act(i)

        @pl.loop(max(first // 4, 1), stop // 4)
        def _(g):
            for u in range(4):
                act(4 * g + u)

    points_copy = pltpu.make_async_copy(points_hbm, points, load_sem.at[0])
    points_copy.start()
    barrier = pltpu.get_barrier_semaphore()
    each_step(
        0,
        owners,
        lambda i: pl.semaphore_signal(
            barrier, inc=1, device_id=device(i), device_id_type=MESH
        ),
    )
    parent_copy = pltpu.make_async_copy(parent_hbm, parent, load_sem.at[1])
    parent_copy.start()
    old_copy = pltpu.make_async_copy(old_hbm, old, load_sem.at[2])
    old_copy.start()
    cent_copies = [
        pltpu.make_async_copy(
            fine_hbm.at[pl.ds(r * size, size)], cent.at[r, pl.ds(0, size)], cent_sem.at[r]
        )
        for r in range(buckets)
    ]
    for copy in cent_copies:
        copy.start()

    n_blocks = bucket_ref.shape[1]
    per_tile = 128 // 2
    column = jnp.transpose(jnp.broadcast_to(bucket_ref[...].astype(F32), (128, n_blocks)))
    lane = iota((1, 128), 1)
    for j in range(n_points // 128):
        own = column[per_tile * j : per_tile * (j + 1)]
        pick = iota((per_tile, 128), 0) == iota((per_tile, 128), 1) // 2
        name = jnp.sum(jnp.where(pick, own, 0.0), axis=0, keepdims=True)
        earlier = iota((n_blocks, 128), 0) < per_tile * j + iota((n_blocks, 128), 1) // 2
        rank = jnp.sum(jnp.where((column == name) & earlier, 1.0, 0.0), axis=0, keepdims=True)
        number = name.astype(jnp.int32)
        step = ((number // buckets - me) * inverse) & (owners - 1)
        code[:, pl.ds(128 * j, 128)] = (
            (number % buckets) * slot_rows
            + step * block_slots
            + rank.astype(jnp.int32) * (block_slots // CAP)
            + (lane & 1)
        )

    points_copy.wait()

    part = 256
    parts = slot_rows // part
    steps_in_part = part // block_slots

    def gather_part(r, c):
        base = r * slot_rows + c * part
        mask = code[...] - base == iota((part, n_points), 0)
        hot = jnp.where(mask, 1.0, 0.0)
        live = jnp.sum(hot, axis=1, keepdims=True)
        rows = dot(hot.astype(BF16), points[...])
        mark = jnp.where((iota((part, 128), 1) == 0) & (live < 0.5), DEAD_MARK, rows[:, :128])
        rows = jnp.concatenate([mark, rows[:, 128:]], axis=1).astype(BF16)
        src[r, pl.ds(c * steps_in_part, steps_in_part)] = rows.reshape(
            steps_in_part, block_slots, width
        )

    def send_part(r, c):
        for q in range(4 // parts):
            first = c * steps_in_part + q * quarter
            each_step(
                first,
                first + quarter,
                lambda i: pltpu.make_async_remote_copy(
                    src_ref=src.at[r, i],
                    dst_ref=dst.at[r, i],
                    send_sem=send_sem.at[r],
                    recv_sem=recv_sem.at[r, first // quarter],
                    device_id=device(i),
                    device_id_type=MESH,
                ).start(),
            )
        if c == 0:
            pltpu.make_async_copy(src.at[r, 0], dst.at[r, 0], recv_sem.at[r, 0]).start()

    def prepare(r):
        cent_copies[r].wait()
        corner = (iota((EXTRA, width), 0) == 0) & (iota((EXTRA, width), 1) == 0)
        cent[r, pl.ds(size, EXTRA)] = jnp.where(corner, 1.0, 0.0).astype(BF16)

        @pl.loop(0, size // 64)
        def _(b):
            rows = pl.ds(pl.multiple_of(b * 64, 64), 64)
            value = cent[r, rows].astype(F32)
            norm = jnp.sum(value * value, axis=1, keepdims=True)
            half_norm[r, rows] = jnp.broadcast_to(0.5 * norm, (64, 128))

    def assign(r, first, steps):
        rows = steps * block_slots
        for q in range(first // quarter, (first + steps) // quarter):
            landed = dst.at[r, pl.ds(q * quarter, quarter)]
            pltpu.make_async_copy(landed, landed, recv_sem.at[r, q]).wait()
        x = dst[r, pl.ds(first, steps)].reshape(rows, width)
        products = dot(cent[r], x, 1, 1)
        live = jnp.where(products[size : size + 1] < 0.75 * DEAD_MARK, 1.0, 0.0)
        norm = jnp.concatenate([half_norm[r]] * (rows // 128), axis=1)
        logits = (products[:size] - norm) * (sharp_ref[r] * width**-0.5)
        shifted = logits - jnp.max(logits, axis=0, keepdims=True)
        exponent = jnp.exp(shifted)
        total = jnp.sum(exponent, axis=0, keepdims=True)
        inverse_total = 1.0 / total
        entropy = jnp.log(total) - jnp.sum(exponent * shifted, axis=0, keepdims=True) * inverse_total
        weights = (exponent * (inverse_total * live)).astype(BF16)
        return x, weights, entropy

    def pack(r, first, entropy):
        held = lane // 32 == r
        for q in range(entropy.shape[1] // 128):
            row = entropy[:, 128 * q : 128 * (q + 1)]
            for g in range(4):
                at = 4 * (first // quarter + q) + g
                turn = (32 * (r - g)) % 128
                moved = pltpu.roll(row, turn, 1) if turn else row
                if r == 0:
                    packed[at] = moved
                else:
                    packed[at] = jnp.where(held, moved, packed[at])

    def weigh(r, first, x, weights):
        weighed = dot(weights, jnp.ones((x.shape[0], 128), BF16))
        weighted = dot(weights, x)
        if first == 0:
            mass[...] = weighed + PRIOR_MASS
            numer[...] = weighted + PRIOR_MASS * cent[r, pl.ds(0, size)].astype(F32)
        else:
            mass[...] += weighed
            numer[...] += weighted

    def member_of(r):
        own = parent[:, pl.ds(r * size, size)] - w * group
        return jnp.where(own == iota((group, size), 0), 1.0, 0.0).astype(BF16)

    def finish(r):
        member = member_of(r)
        high, low = split(mass[...])
        part_mass = dot(member, high) + dot(member, low)
        part_sum = dot(member, numer[...].astype(BF16))
        if r == 0:
            coarse_mass[...] = part_mass
            coarse[...] = part_sum
        else:
            coarse_mass[...] += part_mass
            coarse[...] += part_sum

    def emit(r):
        scale = 1.0 / mass[...]
        for d in range(width // 128):
            cols = pl.ds(128 * d, 128)
            fine_out[pl.ds(r * size, size), cols] = (numer[:, cols] * scale).astype(BF16)

    def whole_bucket(r):
        half = owners // 2
        for first in (0, half):
            x, weights, entropy = assign(r, first, half)
            pack(r, first, entropy)
            weigh(r, first, x, weights)
        finish(r)
        emit(r)

    gather_part(0, 0)
    pl.semaphore_wait(barrier, owners - 1)
    send_part(0, 0)
    for c in range(1, parts):
        gather_part(0, c)
        send_part(0, c)
    for r in range(1, buckets):
        for c in range(parts):
            gather_part(r, c)
            send_part(r, c)
    parent_copy.wait()
    prepare(0)
    prepare(1)
    whole_bucket(0)
    prepare(2)
    whole_bucket(1)
    prepare(3)
    whole_bucket(2)
    each_step(
        0,
        owners,
        lambda i: pltpu.make_async_remote_copy(
            src_ref=packed.at[lax.div(i, 8)],
            dst_ref=packed_back.at[i],
            send_sem=ent_send_sem.at[0],
            recv_sem=ent_recv_sem.at[0],
            device_id=source(i),
            device_id_type=MESH,
        ).start(),
    )
    pltpu.make_async_copy(packed.at[0], packed_back.at[0], ent_recv_sem.at[0]).start()

    def send_entropy(q):
        each_step(
            q * quarter,
            (q + 1) * quarter,
            lambda i: pltpu.make_async_remote_copy(
                src_ref=ent.at[q],
                dst_ref=back.at[i],
                send_sem=ent_send_sem.at[1],
                recv_sem=ent_recv_sem.at[1],
                device_id=source(i),
                device_id_type=MESH,
            ).start(),
        )
        if q == 0:
            pltpu.make_async_copy(ent.at[0], back.at[0], ent_recv_sem.at[1]).start()

    for q in range(3):
        x, weights, entropy = assign(last, q * quarter, quarter)
        ent[q] = entropy
        send_entropy(q)
        weigh(last, q * quarter, x, weights)
    finish(last)
    pltpu.make_async_copy(packed_back, packed_back, ent_recv_sem.at[0]).wait()
    entropy_out[...] = collect(
        packed_back[...].reshape(owners, 128),
        code[...],
        lax.shift_right_logical(code[...] & (slot_rows - 1), 2),
        lambda row: (code[...] < last * slot_rows)
        & (row == 32 * lax.shift_right_logical(code[...], 9) + (code[...] & 31)),
    )

    x, weights, entropy = assign(last, 3 * quarter, quarter)
    ent[3] = entropy
    shares = dot(member_of(last), weights)
    coarse_mass[...] += jnp.sum(shares, axis=1, keepdims=True)
    shares = shares.astype(BF16)

    y, core = lax.div(n, 2), lax.rem(n, 2)
    ys = narrow // 2
    own_rows = group // narrow
    half = width // 2
    core_sends, core_recvs = (core_send0, core_send1), (core_recv0, core_recv1)
    y_sends, y_recvs = (y_send0, y_send1), (y_recv0, y_recv1)

    def tile_of(value):
        high, low = split(value)
        return jnp.where(iota((own_rows, 128), 1) < 64, high.astype(F32), low.astype(F32)).astype(BF16)

    def whole_of(value):
        value = value.astype(F32)
        return value + pltpu.roll(value, 64, 1)

    def rows_of(k, c):
        return pl.ds(pl.multiple_of((2 * k + c) * own_rows, own_rows), own_rows)

    core_copies = []
    for h in range(2):
        cols = pl.ds(h * half, half)
        coarse[:, cols] += dot(shares, x[:, h * half : (h + 1) * half])
        for k in range(ys):
            rows = rows_of(k, 1 - core)
            core_sends[h][k, :, pl.ds(0, half)] = coarse[rows, cols].astype(BF16)
            if h == 0:
                core_sends[h][k, :, pl.ds(half, 128)] = tile_of(coarse_mass[rows])
        copy = pltpu.make_async_remote_copy(
            src_ref=core_sends[h],
            dst_ref=core_recvs[h],
            send_sem=core_send_sem.at[h],
            recv_sem=core_recv_sem.at[h],
            device_id=(w, n + 1 - 2 * core),
            device_id_type=MESH,
        )
        copy.start()
        core_copies.append(copy)
    send_entropy(3)

    def chip_sum(h, k):
        cols = pl.ds(h * half, half)
        rows = rows_of(k, core)
        return coarse[rows, cols] + core_recvs[h][k, :, pl.ds(0, half)].astype(F32)

    def chip_mass(k):
        return coarse_mass[rows_of(k, core)] + whole_of(core_recv0[k, :, pl.ds(half, 128)])

    y_copies = []
    for h in range(2):
        core_copies[h].wait()
        for k in range(1, ys):
            other = lax.rem(y + k, ys)
            y_sends[h][k - 1, :, pl.ds(0, half)] = chip_sum(h, other).astype(BF16)
            if h == 0:
                y_sends[h][k - 1, :, pl.ds(half, 128)] = tile_of(chip_mass(other))
            copy = pltpu.make_async_remote_copy(
                src_ref=y_sends[h].at[k - 1],
                dst_ref=y_recvs[h].at[k - 1],
                send_sem=y_send_sem.at[h, k - 1],
                recv_sem=y_recv_sem.at[h, k - 1],
                device_id=(w, 2 * other + core),
                device_id_type=MESH,
            )
            copy.start()
            y_copies.append(copy)
    weigh(last, 3 * quarter, x, weights)
    emit(last)
    old_copy.wait()
    total = [chip_sum(h, y) for h in range(2)]
    weight = chip_mass(y)
    pltpu.make_async_copy(back, back, ent_recv_sem.at[1]).wait()
    back_out[...] = back[...].reshape(owners, 128)
    for h in range(2):
        for k in range(ys - 1):
            y_copies[h * (ys - 1) + k].wait()
            total[h] = total[h] + y_recvs[h][k, :, pl.ds(0, half)].astype(F32)
            if h == 0:
                weight = weight + whole_of(y_recv0[k, :, pl.ds(half, 128)])
        scale = 0.5 / (weight + PRIOR_MASS)
        for d in range(half // 128):
            cols = pl.ds(h * half + 128 * d, 128)
            here = total[h][:, 128 * d : 128 * (d + 1)]
            coarse_out[:, cols] = (0.5 * old[:, cols].astype(F32) + here * scale).astype(BF16)

    for r in range(buckets):
        sent = src.at[r, pl.ds(0, owners - 1)]
        pltpu.make_async_copy(sent, sent, send_sem.at[r]).wait()
    for k, ref in enumerate((packed_back, back)):
        sent = ref.at[pl.ds(0, owners - 1)]
        pltpu.make_async_copy(sent, sent, ent_send_sem.at[k]).wait()


def close(fine, coarse, entropy, code, back, fine_out, coarse_out, entropy_out, point, sem):
    copies = [
        pltpu.make_async_copy(fine, fine_out, sem.at[0]),
        pltpu.make_async_copy(coarse, coarse_out, sem.at[1]),
    ]
    for copy in copies:
        copy.start()
    held = back.shape[0] * 4
    number = code[...]
    point[...] = entropy[...] + collect(
        back[...],
        number,
        lax.shift_right_logical(number & (held - 1), 2),
        lambda row: (number >= 3 * held) & (row == (number & 127)),
    )
    copies.append(pltpu.make_async_copy(point, entropy_out, sem.at[2]))
    copies[2].start()
    for copy in copies:
        copy.wait()


def body(points, block_bucket, fine, sharp, parents, coarse_old):
    wide, narrow = lax.axis_size("wide"), lax.axis_size("narrow")
    owners = wide * narrow
    n_points, width = points.shape
    n_blocks = block_bucket.shape[0]
    buckets = sharp.shape[0]
    size = fine.shape[0] // buckets
    block_slots = CAP * (n_points // n_blocks)
    own_rows = coarse_old.shape[0]
    group = own_rows * narrow
    ys = narrow // 2
    half = width // 2
    whole = pl.BlockSpec(memory_space=pltpu.VMEM)
    anywhere = pl.BlockSpec(memory_space=pl.ANY)
    in_hbm = pl.BlockSpec(memory_space=pltpu.HBM)
    dma = pltpu.SemaphoreType.DMA
    held = pl.pallas_call(
        functools.partial(kernel, (wide, narrow)),
        out_shape=(
            pltpu.VMEM(fine.shape, BF16),
            pltpu.VMEM(coarse_old.shape, BF16),
            pltpu.VMEM((1, n_points), F32),
            pltpu.VMEM((1, n_points), jnp.int32),
            pltpu.VMEM((owners, 128), F32),
        ),
        in_specs=[pl.BlockSpec(memory_space=pltpu.SMEM), whole] + [in_hbm] * 4,
        out_specs=(whole,) * 5,
        scratch_shapes=[
            pltpu.VMEM((n_points, width), BF16),
            pltpu.VMEM((buckets, size + EXTRA, width), BF16),
            pltpu.VMEM((buckets, size, 128), F32),
            pltpu.VMEM((1, buckets * size), jnp.int32),
            pltpu.VMEM((own_rows, width), BF16),
            pltpu.VMEM((buckets, owners, block_slots, width), BF16),
            pltpu.VMEM((buckets, owners, block_slots, width), BF16),
            pltpu.VMEM((size, width), F32),
            pltpu.VMEM((size, 128), F32),
            pltpu.VMEM((group, width), F32),
            pltpu.VMEM((group, 128), F32),
            pltpu.VMEM((owners // 8, 1, 128), F32),
            pltpu.VMEM((owners, 1, 128), F32),
            pltpu.VMEM((4, 1, 128), F32),
            pltpu.VMEM((owners, 1, 128), F32),
            pltpu.VMEM((ys, own_rows, half + 128), BF16),
            pltpu.VMEM((ys, own_rows, half), BF16),
            pltpu.VMEM((ys, own_rows, half + 128), BF16),
            pltpu.VMEM((ys, own_rows, half), BF16),
            pltpu.VMEM((ys - 1, own_rows, half + 128), BF16),
            pltpu.VMEM((ys - 1, own_rows, half), BF16),
            pltpu.VMEM((ys - 1, own_rows, half + 128), BF16),
            pltpu.VMEM((ys - 1, own_rows, half), BF16),
            dma((3,)),
            dma((buckets,)),
            dma((buckets,)),
            dma((buckets, 4)),
            dma((2,)),
            dma((2,)),
            dma((2,)),
            dma((2,)),
            dma((2, ys - 1)),
            dma((2, ys - 1)),
        ],
        compiler_params=pltpu.CompilerParams(
            collective_id=0, has_side_effects=True, vmem_limit_bytes=48 << 20
        ),
    )(
        sharp,
        block_bucket.reshape(1, n_blocks),
        *[
            pltpu.with_memory_space_constraint(value, pltpu.HBM)
            for value in (parents.reshape(1, buckets * size), points, fine, coarse_old)
        ],
    )
    fine_new, coarse_new, entropy = pl.pallas_call(
        close,
        out_shape=(
            jax.ShapeDtypeStruct(fine.shape, BF16),
            jax.ShapeDtypeStruct(coarse_old.shape, BF16),
            jax.ShapeDtypeStruct((1, n_points), F32),
        ),
        in_specs=[whole] * 5,
        out_specs=(anywhere,) * 3,
        scratch_shapes=[pltpu.VMEM((1, n_points), F32), dma((3,))],
        compiler_params=pltpu.CompilerParams(vmem_limit_bytes=16 << 20),
    )(*[pltpu.with_memory_space_constraint(value, pltpu.VMEM) for value in held])
    return fine_new, coarse_new, entropy.reshape(n_points)


def solution(mesh):
    both = ("wide", "narrow")
    return jax.shard_map(
        body,
        mesh=mesh,
        in_specs=(P(both, None), P(both), P(both, None), P(both), P(both), P(both, None)),
        out_specs=(P(both, None), P(both, None), P(both)),
        check_vma=False,
    )
```

time: 90.8 us -> 75.8 us (0.83)
  Pallas kernels: 84.1 us -> 73.5 us
  local copies, waits for them, and re-layouts: 5.9 us -> 1.33 us
    pallas_call x1 -> x2, Pallas kernels: 84.1 us -> 73.5 us  [the longest x1 71.4 us: body(): pl.pallas_call(functools.partial(kernel, (wide, narrow)), out_shape=(pltp...]
    unnamed x7 -> x4, local copies, waits for them, and re-layouts: 5.9 us -> 1.33 us
where the time goes in v2:
time: 75.8 us; the launch traced here: 75.6 us
  Pallas kernels  73.5 us (97%)
  local copies, waits for them, and re-layouts  1.33 us (2%)
  between operations  0.81 us (1%)
    pallas_call x1, Pallas kernels, body(): pl.pallas_call(functools.partial(kernel, (wide, narrow)), out_shape=(pltp...  71.4 us
    pallas_call x1, Pallas kernels, body(): pl.pallas_call(close, out_shape=(jax.ShapeDtypeStruct(fine.shape, BF16),...  2.05 us

profile of v2, /device:TPU:1, one launch (start us, length us, event | category | flops | bytes accessed | tf_op | source)
XLA Modules:
  0.0 75.6 jit_solution(9114064837222025985)
XLA Ops:
  0.6 0.0 copy-start
  0.6 0.7 copy-done
  1.3 0.0 copy-start.1
  1.3 0.7 copy-done.1
  2.0 71.4 %shard_map.85 = (bf16[2048,1024]{1,0:T(8,128)(2,1)S(1)}, bf16[32,1024]{1,0:T(8,128)(2,1)S(1)}, f32[1,1024]{1,0:T(1,128)S(1)}, s32[1,1024]{1,0:T(1,128)S(1)}, f32[128,128]{1,0:T(8,128)S(1)}) custom-call(f32[4]{0:T(128)S(1)} %copy-done.1, s32[1,512]{1,0:T(1,128)S(1)} %bitcast.3, s32[1,2048]{1,0:T(1,128)} %bitcast.4, bf16[1024,1024]{1,0:T(8,128)(2,1)} %points_hbm.1, ...), custom_call_target="tpu_custom_call" | custom-call | tf_op jit(solution)/shard_map/pallas_call | solution.py:481
  73.4 2.0 %shard_map.86 = (bf16[2048,1024]{1,0:T(8,128)(2,1)}, bf16[32,1024]{1,0:T(8,128)(2,1)}, f32[1,1024]{1,0:T(1,128)}) custom-call(bf16[2048,1024]{1,0:T(8,128)(2,1)S(1)} %get-tuple-element.11.fine, bf16[32,1024]{1,0:T(8,128)(2,1)S(1)} %get-tuple-element.12.coarse, f32[1,1024]{1,0:T(1,128)S(1)} %get-tuple-element.13.entropy, ...), custom_call_target="tpu_custom_call" | custom-call | tf_op jit(solution)/shard_map/pallas_call | solution.py:538
Async XLA Ops:
  0.6 0.7 copy-start
  1.3 0.7 copy-start.1

commit v3 on v2

--- a/solution.py
+++ b/solution.py
@@ -31,19 +31,10 @@
     return high, (value - high.astype(F32)).astype(BF16)
 
 
-def collect(found_in, code, place, mine_of):
-    owners, n_points = found_in.shape[0], code.shape[1]
-    high, low = split(found_in)
-    hot = jnp.where(place == iota((owners, n_points), 0), 1.0, 0.0).astype(BF16)
-    found = dot(high, hot, 0, 0) + dot(low, hot, 0, 0)
-    mine = mine_of(iota((128, n_points), 0))
-    return jnp.sum(jnp.where(mine, found, 0.0), axis=0, keepdims=True)
-
-
 def kernel(
     dims,
-    sharp_ref,
-    bucket_ref,
+    sharp_hbm,
+    bucket_hbm,
     parent_hbm,
     points_hbm,
     fine_hbm,
@@ -51,8 +42,9 @@
     fine_out,
     coarse_out,
     entropy_out,
+    sharp_ref,
+    bucket_ref,
     code,
-    back_out,
     points,
     cent,
     half_norm,
@@ -65,8 +57,6 @@
     coarse,
     coarse_mass,
     packed,
-    packed_back,
-    ent,
     back,
     core_send0,
     core_send1,
@@ -80,8 +70,7 @@
     cent_sem,
     send_sem,
     recv_sem,
-    ent_send_sem,
-    ent_recv_sem,
+    ent_sem,
     core_send_sem,
     core_recv_sem,
     y_send_sem,
@@ -118,6 +107,8 @@
             for u in range(4):
                 act(4 * g + u)
 
+    bucket_copy = pltpu.make_async_copy(bucket_hbm, bucket_ref, load_sem.at[3])
+    bucket_copy.start()
     points_copy = pltpu.make_async_copy(points_hbm, points, load_sem.at[0])
     points_copy.start()
     barrier = pltpu.get_barrier_semaphore()
@@ -128,6 +119,8 @@
             barrier, inc=1, device_id=device(i), device_id_type=MESH
         ),
     )
+    sharp_copy = pltpu.make_async_copy(sharp_hbm, sharp_ref, load_sem.at[4])
+    sharp_copy.start()
     parent_copy = pltpu.make_async_copy(parent_hbm, parent, load_sem.at[1])
     parent_copy.start()
     old_copy = pltpu.make_async_copy(old_hbm, old, load_sem.at[2])
@@ -143,6 +136,7 @@
 
     n_blocks = bucket_ref.shape[1]
     per_tile = 128 // 2
+    bucket_copy.wait()
     column = jnp.transpose(jnp.broadcast_to(bucket_ref[...].astype(F32), (128, n_blocks)))
     lane = iota((1, 128), 1)
     for j in range(n_points // 128):
@@ -162,38 +156,30 @@
 
     points_copy.wait()
 
-    part = 256
-    parts = slot_rows // part
-    steps_in_part = part // block_slots
-
-    def gather_part(r, c):
-        base = r * slot_rows + c * part
-        mask = code[...] - base == iota((part, n_points), 0)
+    def gather_part(r, first, steps):
+        rows = steps * block_slots
+        mask = code[...] - (r * slot_rows + first * block_slots) == iota((rows, n_points), 0)
         hot = jnp.where(mask, 1.0, 0.0)
         live = jnp.sum(hot, axis=1, keepdims=True)
-        rows = dot(hot.astype(BF16), points[...])
-        mark = jnp.where((iota((part, 128), 1) == 0) & (live < 0.5), DEAD_MARK, rows[:, :128])
-        rows = jnp.concatenate([mark, rows[:, 128:]], axis=1).astype(BF16)
-        src[r, pl.ds(c * steps_in_part, steps_in_part)] = rows.reshape(
-            steps_in_part, block_slots, width
+        found = dot(hot.astype(BF16), points[...])
+        mark = jnp.where((iota((rows, 128), 1) == 0) & (live < 0.5), DEAD_MARK, found[:, :128])
+        found = jnp.concatenate([mark, found[:, 128:]], axis=1).astype(BF16)
+        src[r, pl.ds(first, steps)] = found.reshape(steps, block_slots, width)
+
+    def send_part(r, q):
+        each_step(
+            q * quarter,
+            (q + 1) * quarter,
+            lambda i: pltpu.make_async_remote_copy(
+                src_ref=src.at[r, i],
+                dst_ref=dst.at[r, i],
+                send_sem=send_sem.at[r],
+                recv_sem=recv_sem.at[r, q],
+                device_id=device(i),
+                device_id_type=MESH,
+            ).start(),
         )
-
-    def send_part(r, c):
-        for q in range(4 // parts):
-            first = c * steps_in_part + q * quarter
-            each_step(
-                first,
-                first + quarter,
-                lambda i: pltpu.make_async_remote_copy(
-                    src_ref=src.at[r, i],
-                    dst_ref=dst.at[r, i],
-                    send_sem=send_sem.at[r],
-                    recv_sem=recv_sem.at[r, first // quarter],
-                    device_id=device(i),
-                    device_id_type=MESH,
-                ).start(),
-            )
-        if c == 0:
+        if q == 0:
             pltpu.make_async_copy(src.at[r, 0], dst.at[r, 0], recv_sem.at[r, 0]).start()
 
     def prepare(r):
@@ -217,7 +203,7 @@
         products = dot(cent[r], x, 1, 1)
         live = jnp.where(products[size : size + 1] < 0.75 * DEAD_MARK, 1.0, 0.0)
         norm = jnp.concatenate([half_norm[r]] * (rows // 128), axis=1)
-        logits = (products[:size] - norm) * (sharp_ref[r] * width**-0.5)
+        logits = (products[:size] - norm) * (sharp_ref[0, r] * width**-0.5)
         shifted = logits - jnp.max(logits, axis=0, keepdims=True)
         exponent = jnp.exp(shifted)
         total = jnp.sum(exponent, axis=0, keepdims=True)
@@ -280,16 +266,18 @@
         finish(r)
         emit(r)
 
-    gather_part(0, 0)
+    gather_part(0, 0, quarter)
     pl.semaphore_wait(barrier, owners - 1)
     send_part(0, 0)
-    for c in range(1, parts):
-        gather_part(0, c)
-        send_part(0, c)
+    for q in range(1, 4):
+        gather_part(0, q * quarter, quarter)
+        send_part(0, q)
     for r in range(1, buckets):
-        for c in range(parts):
-            gather_part(r, c)
-            send_part(r, c)
+        for q in (0, 2):
+            gather_part(r, q * quarter, 2 * quarter)
+            send_part(r, q)
+            send_part(r, q + 1)
+    sharp_copy.wait()
     parent_copy.wait()
     prepare(0)
     prepare(1)
@@ -298,53 +286,31 @@
     whole_bucket(1)
     prepare(3)
     whole_bucket(2)
-    each_step(
-        0,
-        owners,
-        lambda i: pltpu.make_async_remote_copy(
-            src_ref=packed.at[lax.div(i, 8)],
-            dst_ref=packed_back.at[i],
-            send_sem=ent_send_sem.at[0],
-            recv_sem=ent_recv_sem.at[0],
-            device_id=source(i),
-            device_id_type=MESH,
-        ).start(),
-    )
-    pltpu.make_async_copy(packed.at[0], packed_back.at[0], ent_recv_sem.at[0]).start()
 
     def send_entropy(q):
         each_step(
             q * quarter,
             (q + 1) * quarter,
             lambda i: pltpu.make_async_remote_copy(
-                src_ref=ent.at[q],
+                src_ref=packed.at[lax.div(i, 8)],
                 dst_ref=back.at[i],
-                send_sem=ent_send_sem.at[1],
-                recv_sem=ent_recv_sem.at[1],
+                send_sem=ent_sem.at[0],
+                recv_sem=ent_sem.at[1],
                 device_id=source(i),
                 device_id_type=MESH,
             ).start(),
         )
         if q == 0:
-            pltpu.make_async_copy(ent.at[0], back.at[0], ent_recv_sem.at[1]).start()
+            pltpu.make_async_copy(packed.at[0], back.at[0], ent_sem.at[1]).start()
 
     for q in range(3):
         x, weights, entropy = assign(last, q * quarter, quarter)
-        ent[q] = entropy
+        pack(last, q * quarter, entropy)
         send_entropy(q)
         weigh(last, q * quarter, x, weights)
     finish(last)
-    pltpu.make_async_copy(packed_back, packed_back, ent_recv_sem.at[0]).wait()
-    entropy_out[...] = collect(
-        packed_back[...].reshape(owners, 128),
-        code[...],
-        lax.shift_right_logical(code[...] & (slot_rows - 1), 2),
-        lambda row: (code[...] < last * slot_rows)
-        & (row == 32 * lax.shift_right_logical(code[...], 9) + (code[...] & 31)),
-    )
 
     x, weights, entropy = assign(last, 3 * quarter, quarter)
-    ent[3] = entropy
     shares = dot(member_of(last), weights)
     coarse_mass[...] += jnp.sum(shares, axis=1, keepdims=True)
     shares = shares.astype(BF16)
@@ -386,6 +352,7 @@
         )
         copy.start()
         core_copies.append(copy)
+    pack(last, 3 * quarter, entropy)
     send_entropy(3)
 
     def chip_sum(h, k):
@@ -419,8 +386,15 @@
     old_copy.wait()
     total = [chip_sum(h, y) for h in range(2)]
     weight = chip_mass(y)
-    pltpu.make_async_copy(back, back, ent_recv_sem.at[1]).wait()
-    back_out[...] = back[...].reshape(owners, 128)
+    pltpu.make_async_copy(back, back, ent_sem.at[1]).wait()
+    high, low = split(back[...].reshape(owners, 128))
+    number = code[...]
+    place = lax.shift_right_logical(number & (slot_rows - 1), 2)
+    hot = jnp.where(place == iota((owners, n_points), 0), 1.0, 0.0).astype(BF16)
+    found = dot(high, hot, 0, 0) + dot(low, hot, 0, 0)
+    spot = 32 * lax.shift_right_logical(number, 9) + (number & 31)
+    mine = spot == iota((128, n_points), 0)
+    entropy_out[...] = jnp.sum(jnp.where(mine, found, 0.0), axis=0, keepdims=True)
     for h in range(2):
         for k in range(ys - 1):
             y_copies[h * (ys - 1) + k].wait()
@@ -436,28 +410,23 @@
     for r in range(buckets):
         sent = src.at[r, pl.ds(0, owners - 1)]
         pltpu.make_async_copy(sent, sent, send_sem.at[r]).wait()
-    for k, ref in enumerate((packed_back, back)):
-        sent = ref.at[pl.ds(0, owners - 1)]
-        pltpu.make_async_copy(sent, sent, ent_send_sem.at[k]).wait()
-
-
-def close(fine, coarse, entropy, code, back, fine_out, coarse_out, entropy_out, point, sem):
+    sent = back.at[pl.ds(0, owners - 1)]
+    pltpu.make_async_copy(sent, sent, ent_sem.at[0]).wait()
+
+
+def close(fine, coarse, entropy, fine_out, coarse_out, entropy_out, sem):
+    pieces = 8
+    rows = fine.shape[0] // pieces
     copies = [
-        pltpu.make_async_copy(fine, fine_out, sem.at[0]),
-        pltpu.make_async_copy(coarse, coarse_out, sem.at[1]),
+        pltpu.make_async_copy(
+            fine.at[pl.ds(k * rows, rows)], fine_out.at[pl.ds(k * rows, rows)], sem.at[k]
+        )
+        for k in range(pieces)
     ]
+    copies.append(pltpu.make_async_copy(coarse, coarse_out, sem.at[pieces]))
+    copies.append(pltpu.make_async_copy(entropy, entropy_out, sem.at[pieces + 1]))
     for copy in copies:
         copy.start()
-    held = back.shape[0] * 4
-    number = code[...]
-    point[...] = entropy[...] + collect(
-        back[...],
-        number,
-        lax.shift_right_logical(number & (held - 1), 2),
-        lambda row: (number >= 3 * held) & (row == (number & 127)),
-    )
-    copies.append(pltpu.make_async_copy(point, entropy_out, sem.at[2]))
-    copies[2].start()
     for copy in copies:
         copy.wait()
 
@@ -484,12 +453,13 @@
             pltpu.VMEM(fine.shape, BF16),
             pltpu.VMEM(coarse_old.shape, BF16),
             pltpu.VMEM((1, n_points), F32),
+        ),
+        in_specs=[in_hbm] * 6,
+        out_specs=(whole,) * 3,
+        scratch_shapes=[
+            pltpu.SMEM((1, buckets), F32),
+            pltpu.VMEM((1, n_blocks), jnp.int32),
             pltpu.VMEM((1, n_points), jnp.int32),
-            pltpu.VMEM((owners, 128), F32),
-        ),
-        in_specs=[pl.BlockSpec(memory_space=pltpu.SMEM), whole] + [in_hbm] * 4,
-        out_specs=(whole,) * 5,
-        scratch_shapes=[
             pltpu.VMEM((n_points, width), BF16),
             pltpu.VMEM((buckets, size + EXTRA, width), BF16),
             pltpu.VMEM((buckets, size, 128), F32),
@@ -503,8 +473,6 @@
             pltpu.VMEM((group, 128), F32),
             pltpu.VMEM((owners // 8, 1, 128), F32),
             pltpu.VMEM((owners, 1, 128), F32),
-            pltpu.VMEM((4, 1, 128), F32),
-            pltpu.VMEM((owners, 1, 128), F32),
             pltpu.VMEM((ys, own_rows, half + 128), BF16),
             pltpu.VMEM((ys, own_rows, half), BF16),
             pltpu.VMEM((ys, own_rows, half + 128), BF16),
@@ -513,11 +481,10 @@
             pltpu.VMEM((ys - 1, own_rows, half), BF16),
             pltpu.VMEM((ys - 1, own_rows, half + 128), BF16),
             pltpu.VMEM((ys - 1, own_rows, half), BF16),
-            dma((3,)),
+            dma((5,)),
             dma((buckets,)),
             dma((buckets,)),
             dma((buckets, 4)),
-            dma((2,)),
             dma((2,)),
             dma((2,)),
             dma((2,)),
@@ -528,11 +495,16 @@
             collective_id=0, has_side_effects=True, vmem_limit_bytes=48 << 20
         ),
     )(
-        sharp,
-        block_bucket.reshape(1, n_blocks),
         *[
             pltpu.with_memory_space_constraint(value, pltpu.HBM)
-            for value in (parents.reshape(1, buckets * size), points, fine, coarse_old)
+            for value in (
+                sharp.reshape(1, buckets),
+                block_bucket.reshape(1, n_blocks),
+                parents.reshape(1, buckets * size),
+                points,
+                fine,
+                coarse_old,
+            )
         ],
     )
     fine_new, coarse_new, entropy = pl.pallas_call(
@@ -542,9 +514,9 @@
             jax.ShapeDtypeStruct(coarse_old.shape, BF16),
             jax.ShapeDtypeStruct((1, n_points), F32),
         ),
-        in_specs=[whole] * 5,
+        in_specs=[whole] * 3,
         out_specs=(anywhere,) * 3,
-        scratch_shapes=[pltpu.VMEM((1, n_points), F32), dma((3,))],
+        scratch_shapes=[dma((10,))],
         compiler_params=pltpu.CompilerParams(vmem_limit_bytes=16 << 20),
     )(*[pltpu.with_memory_space_constraint(value, pltpu.VMEM) for value in held])
     return fine_new, coarse_new, entropy.reshape(n_points)

time: 75.8 us -> 72.6 us (0.958)
  Pallas kernels: 73.5 us -> 71.7 us
  local copies, waits for them, and re-layouts: 1.33 us -> 0 us
    pallas_call x1, Pallas kernels: 71.4 us -> 69.6 us  [body(): pl.pallas_call(functools.partial(kernel, (wide, narrow)), out_shape=(pltp...]
    unnamed x4 -> x0, local copies, waits for them, and re-layouts: 1.33 us -> none
where the time goes in v3:
time: 72.6 us; the launch traced here: 72.5 us
  Pallas kernels  71.7 us (99%)
  between operations  0.8 us (1%)
    pallas_call x1, Pallas kernels, body(): pl.pallas_call(functools.partial(kernel, (wide, narrow)), out_shape=(pltp...  69.6 us
    pallas_call x1, Pallas kernels, body(): pl.pallas_call(close, out_shape=(jax.ShapeDtypeStruct(fine.shape, BF16),...  2.1 us

profile of v3, /device:TPU:1, one launch (start us, length us, event | category | flops | bytes accessed | tf_op | source)
XLA Modules:
  0.0 72.5 jit_solution(5919121935312682793)
XLA Ops:
  0.6 69.6 %shard_map.85 = (bf16[2048,1024]{1,0:T(8,128)(2,1)S(1)}, bf16[32,1024]{1,0:T(8,128)(2,1)S(1)}, f32[1,1024]{1,0:T(1,128)S(1)}) custom-call(f32[1,4]{1,0:T(1,128)} %bitcast.6, s32[1,512]{1,0:T(1,128)} %bitcast.5, s32[1,2048]{1,0:T(1,128)} %bitcast.4, bf16[1024,1024]{1,0:T(8,128)(2,1)} %points_hbm.1, bf16[2048,1024]{1,0:T(8,128)(2,1)} %fine_hbm.1, ...), custom_call_target="tpu_custom_call" | custom-call | tf_op jit(solution)/shard_map/pallas_call | solution.py:450
  70.2 2.1 %shard_map.86 = (bf16[2048,1024]{1,0:T(8,128)(2,1)}, bf16[32,1024]{1,0:T(8,128)(2,1)}, f32[1,1024]{1,0:T(1,128)}) custom-call(bf16[2048,1024]{1,0:T(8,128)(2,1)S(1)} %get-tuple-element.9.fine, bf16[32,1024]{1,0:T(8,128)(2,1)S(1)} %get-tuple-element.10.coarse, f32[1,1024]{1,0:T(1,128)S(1)} %get-tuple-element.11.entropy), custom_call_target="tpu_custom_call" | custom-call | tf_op jit(solution)/shard_map/pallas_call | solution.py:510

commit v4 on v3

--- a/solution.py
+++ b/solution.py
@@ -13,7 +13,7 @@
 
 CAP = 2
 PRIOR_MASS = 1.0
-STRIDE = 37
+STRIDE = 91
 DEAD_MARK = 16.0
 EXTRA = 16
 
@@ -38,18 +38,17 @@
     parent_hbm,
     points_hbm,
     fine_hbm,
-    old_hbm,
     fine_out,
-    coarse_out,
-    entropy_out,
+    total_out,
+    weight_out,
+    code,
+    back_out,
     sharp_ref,
     bucket_ref,
-    code,
     points,
     cent,
     half_norm,
     parent,
-    old,
     src,
     dst,
     numer,
@@ -107,7 +106,7 @@
             for u in range(4):
                 act(4 * g + u)
 
-    bucket_copy = pltpu.make_async_copy(bucket_hbm, bucket_ref, load_sem.at[3])
+    bucket_copy = pltpu.make_async_copy(bucket_hbm, bucket_ref, load_sem.at[2])
     bucket_copy.start()
     points_copy = pltpu.make_async_copy(points_hbm, points, load_sem.at[0])
     points_copy.start()
@@ -119,21 +118,6 @@
             barrier, inc=1, device_id=device(i), device_id_type=MESH
         ),
     )
-    sharp_copy = pltpu.make_async_copy(sharp_hbm, sharp_ref, load_sem.at[4])
-    sharp_copy.start()
-    parent_copy = pltpu.make_async_copy(parent_hbm, parent, load_sem.at[1])
-    parent_copy.start()
-    old_copy = pltpu.make_async_copy(old_hbm, old, load_sem.at[2])
-    old_copy.start()
-    cent_copies = [
-        pltpu.make_async_copy(
-            fine_hbm.at[pl.ds(r * size, size)], cent.at[r, pl.ds(0, size)], cent_sem.at[r]
-        )
-        for r in range(buckets)
-    ]
-    for copy in cent_copies:
-        copy.start()
-
     n_blocks = bucket_ref.shape[1]
     per_tile = 128 // 2
     bucket_copy.wait()
@@ -143,8 +127,10 @@
         own = column[per_tile * j : per_tile * (j + 1)]
         pick = iota((per_tile, 128), 0) == iota((per_tile, 128), 1) // 2
         name = jnp.sum(jnp.where(pick, own, 0.0), axis=0, keepdims=True)
-        earlier = iota((n_blocks, 128), 0) < per_tile * j + iota((n_blocks, 128), 1) // 2
-        rank = jnp.sum(jnp.where((column == name) & earlier, 1.0, 0.0), axis=0, keepdims=True)
+        upto = per_tile * (j + 1)
+        earlier = iota((upto, 128), 0) < per_tile * j + iota((upto, 128), 1) // 2
+        same = (column[:upto] == name) & earlier
+        rank = jnp.sum(jnp.where(same, 1.0, 0.0), axis=0, keepdims=True)
         number = name.astype(jnp.int32)
         step = ((number // buckets - me) * inverse) & (owners - 1)
         code[:, pl.ds(128 * j, 128)] = (
@@ -269,6 +255,18 @@
     gather_part(0, 0, quarter)
     pl.semaphore_wait(barrier, owners - 1)
     send_part(0, 0)
+    sharp_copy = pltpu.make_async_copy(sharp_hbm, sharp_ref, load_sem.at[3])
+    sharp_copy.start()
+    parent_copy = pltpu.make_async_copy(parent_hbm, parent, load_sem.at[1])
+    parent_copy.start()
+    cent_copies = [
+        pltpu.make_async_copy(
+            fine_hbm.at[pl.ds(r * size, size)], cent.at[r, pl.ds(0, size)], cent_sem.at[r]
+        )
+        for r in range(buckets)
+    ]
+    for copy in cent_copies:
+        copy.start()
     for q in range(1, 4):
         gather_part(0, q * quarter, quarter)
         send_part(0, q)
@@ -310,8 +308,9 @@
         weigh(last, q * quarter, x, weights)
     finish(last)
 
+    member = member_of(last)
     x, weights, entropy = assign(last, 3 * quarter, quarter)
-    shares = dot(member_of(last), weights)
+    shares = dot(member, weights)
     coarse_mass[...] += jnp.sum(shares, axis=1, keepdims=True)
     shares = shares.astype(BF16)
 
@@ -366,7 +365,7 @@
     y_copies = []
     for h in range(2):
         core_copies[h].wait()
-        for k in range(1, ys):
+        for k in (2, 1, 3):
             other = lax.rem(y + k, ys)
             y_sends[h][k - 1, :, pl.ds(0, half)] = chip_sum(h, other).astype(BF16)
             if h == 0:
@@ -383,29 +382,19 @@
             y_copies.append(copy)
     weigh(last, 3 * quarter, x, weights)
     emit(last)
-    old_copy.wait()
     total = [chip_sum(h, y) for h in range(2)]
     weight = chip_mass(y)
-    pltpu.make_async_copy(back, back, ent_sem.at[1]).wait()
-    high, low = split(back[...].reshape(owners, 128))
-    number = code[...]
-    place = lax.shift_right_logical(number & (slot_rows - 1), 2)
-    hot = jnp.where(place == iota((owners, n_points), 0), 1.0, 0.0).astype(BF16)
-    found = dot(high, hot, 0, 0) + dot(low, hot, 0, 0)
-    spot = 32 * lax.shift_right_logical(number, 9) + (number & 31)
-    mine = spot == iota((128, n_points), 0)
-    entropy_out[...] = jnp.sum(jnp.where(mine, found, 0.0), axis=0, keepdims=True)
     for h in range(2):
         for k in range(ys - 1):
             y_copies[h * (ys - 1) + k].wait()
+        for k in range(ys - 1):
             total[h] = total[h] + y_recvs[h][k, :, pl.ds(0, half)].astype(F32)
             if h == 0:
                 weight = weight + whole_of(y_recv0[k, :, pl.ds(half, 128)])
-        scale = 0.5 / (weight + PRIOR_MASS)
-        for d in range(half // 128):
-            cols = pl.ds(h * half + 128 * d, 128)
-            here = total[h][:, 128 * d : 128 * (d + 1)]
-            coarse_out[:, cols] = (0.5 * old[:, cols].astype(F32) + here * scale).astype(BF16)
+        total_out[:, pl.ds(h * half, half)] = total[h]
+    weight_out[...] = weight
+    pltpu.make_async_copy(back, back, ent_sem.at[1]).wait()
+    back_out[...] = back[...].reshape(owners, 128)
 
     for r in range(buckets):
         sent = src.at[r, pl.ds(0, owners - 1)]
@@ -414,21 +403,31 @@
     pltpu.make_async_copy(sent, sent, ent_sem.at[0]).wait()
 
 
-def close(fine, coarse, entropy, fine_out, coarse_out, entropy_out, sem):
-    pieces = 8
-    rows = fine.shape[0] // pieces
-    copies = [
-        pltpu.make_async_copy(
-            fine.at[pl.ds(k * rows, rows)], fine_out.at[pl.ds(k * rows, rows)], sem.at[k]
-        )
-        for k in range(pieces)
-    ]
-    copies.append(pltpu.make_async_copy(coarse, coarse_out, sem.at[pieces]))
-    copies.append(pltpu.make_async_copy(entropy, entropy_out, sem.at[pieces + 1]))
-    for copy in copies:
-        copy.start()
-    for copy in copies:
-        copy.wait()
+def close(
+    fine, total, weight, code, back, old, fine_out, coarse_out, entropy_out, coarse, point, sem
+):
+    fine_copy = pltpu.make_async_copy(fine, fine_out, sem.at[0])
+    fine_copy.start()
+    scale = 0.5 / (weight[...] + PRIOR_MASS)
+    for d in range(total.shape[1] // 128):
+        cols = pl.ds(128 * d, 128)
+        coarse[:, cols] = (0.5 * old[:, cols].astype(F32) + total[:, cols] * scale).astype(BF16)
+    coarse_copy = pltpu.make_async_copy(coarse, coarse_out, sem.at[1])
+    coarse_copy.start()
+    owners, n_points = back.shape[0], code.shape[1]
+    high, low = split(back[...])
+    number = code[...]
+    place = lax.shift_right_logical(number, 2) & (owners - 1)
+    hot = jnp.where(place == iota((owners, n_points), 0), 1.0, 0.0).astype(BF16)
+    found = dot(high, hot, 0, 0) + dot(low, hot, 0, 0)
+    spot = 32 * lax.shift_right_logical(number, 9) + (number & 31)
+    mine = spot == iota((128, n_points), 0)
+    point[...] = jnp.sum(jnp.where(mine, found, 0.0), axis=0, keepdims=True)
+    point_copy = pltpu.make_async_copy(point, entropy_out, sem.at[2])
+    point_copy.start()
+    coarse_copy.wait()
+    point_copy.wait()
+    fine_copy.wait()
 
 
 def body(points, block_bucket, fine, sharp, parents, coarse_old):
@@ -451,20 +450,20 @@
         functools.partial(kernel, (wide, narrow)),
         out_shape=(
             pltpu.VMEM(fine.shape, BF16),
-            pltpu.VMEM(coarse_old.shape, BF16),
-            pltpu.VMEM((1, n_points), F32),
+            pltpu.VMEM(coarse_old.shape, F32),
+            pltpu.VMEM((own_rows, 128), F32),
+            pltpu.VMEM((1, n_points), jnp.int32),
+            pltpu.VMEM((owners, 128), F32),
         ),
-        in_specs=[in_hbm] * 6,
-        out_specs=(whole,) * 3,
+        in_specs=[in_hbm] * 5,
+        out_specs=(whole,) * 5,
         scratch_shapes=[
             pltpu.SMEM((1, buckets), F32),
             pltpu.VMEM((1, n_blocks), jnp.int32),
-            pltpu.VMEM((1, n_points), jnp.int32),
             pltpu.VMEM((n_points, width), BF16),
             pltpu.VMEM((buckets, size + EXTRA, width), BF16),
             pltpu.VMEM((buckets, size, 128), F32),
             pltpu.VMEM((1, buckets * size), jnp.int32),
-            pltpu.VMEM((own_rows, width), BF16),
             pltpu.VMEM((buckets, owners, block_slots, width), BF16),
             pltpu.VMEM((buckets, owners, block_slots, width), BF16),
             pltpu.VMEM((size, width), F32),
@@ -481,7 +480,7 @@
             pltpu.VMEM((ys - 1, own_rows, half), BF16),
             pltpu.VMEM((ys - 1, own_rows, half + 128), BF16),
             pltpu.VMEM((ys - 1, own_rows, half), BF16),
-            dma((5,)),
+            dma((4,)),
             dma((buckets,)),
             dma((buckets,)),
             dma((buckets, 4)),
@@ -503,7 +502,6 @@
                 parents.reshape(1, buckets * size),
                 points,
                 fine,
-                coarse_old,
             )
         ],
     )
@@ -514,11 +512,15 @@
             jax.ShapeDtypeStruct(coarse_old.shape, BF16),
             jax.ShapeDtypeStruct((1, n_points), F32),
         ),
-        in_specs=[whole] * 3,
+        in_specs=[whole] * 6,
         out_specs=(anywhere,) * 3,
-        scratch_shapes=[dma((10,))],
+        scratch_shapes=[
+            pltpu.VMEM(coarse_old.shape, BF16),
+            pltpu.VMEM((1, n_points), F32),
+            dma((3,)),
+        ],
         compiler_params=pltpu.CompilerParams(vmem_limit_bytes=16 << 20),
-    )(*[pltpu.with_memory_space_constraint(value, pltpu.VMEM) for value in held])
+    )(*[pltpu.with_memory_space_constraint(value, pltpu.VMEM) for value in (*held, coarse_old)])
     return fine_new, coarse_new, entropy.reshape(n_points)
 
 

time: 72.6 us -> 72.2 us (level)
  no operation moved by 1% of the time
where the time goes in v4:
time: 72.2 us; the launch traced here: 72.1 us
  Pallas kernels  71.3 us (99%)
  between operations  0.82 us (1%)
    pallas_call x1, Pallas kernels, body(): pl.pallas_call(functools.partial(kernel, (wide, narrow)), out_shape=(pltp...  69.2 us
    pallas_call x1, Pallas kernels, body(): pl.pallas_call(close, out_shape=(jax.ShapeDtypeStruct(fine.shape, BF16),...  2.04 us

profile of v4, /device:TPU:1, one launch (start us, length us, event | category | flops | bytes accessed | tf_op | source)
XLA Modules:
  0.0 72.1 jit_solution(3235665875566496929)
XLA Ops:
  0.6 0.0 copy-start
  0.6 69.2 %shard_map.85 = (bf16[2048,1024]{1,0:T(8,128)(2,1)S(1)}, f32[32,1024]{1,0:T(8,128)S(1)}, f32[32,128]{1,0:T(8,128)S(1)}, s32[1,1024]{1,0:T(1,128)S(1)}, f32[128,128]{1,0:T(8,128)S(1)}) custom-call(f32[1,4]{1,0:T(1,128)} %bitcast.6, s32[1,512]{1,0:T(1,128)} %bitcast.5, s32[1,2048]{1,0:T(1,128)} %bitcast.4, bf16[1024,1024]{1,0:T(8,128)(2,1)} %points_hbm.1, ...), custom_call_target="tpu_custom_call" | custom-call | tf_op jit(solution)/shard_map/pallas_call | solution.py:449
  69.9 0.0 copy-done
  69.9 2.0 %shard_map.86 = (bf16[2048,1024]{1,0:T(8,128)(2,1)}, bf16[32,1024]{1,0:T(8,128)(2,1)}, f32[1,1024]{1,0:T(1,128)}) custom-call(bf16[2048,1024]{1,0:T(8,128)(2,1)S(1)} %get-tuple-element.11.fine, f32[32,1024]{1,0:T(8,128)S(1)} %get-tuple-element.12.total, f32[32,128]{1,0:T(8,128)S(1)} %get-tuple-element.13.weight, s32[1,1024]{1,0:T(1,128)S(1)} %get-tuple-element.14.code, ...), custom_call_target="tpu_custom_call" | custom-call | tf_op jit(solution)/shard_map/pallas_call | solution.py:508
Async XLA Ops:
  0.6 69.3 %copy-start = (bf16[32,1024]{1,0:T(8,128)(2,1)S(1)}, bf16[32,1024]{1,0:T(8,128)(2,1)}, u32[]{:S(2)}) copy-start(bf16[32,1024]{1,0:T(8,128)(2,1)} %old.1) | copy-start | bytes 196612
